TPU v7x, 32 devices: a whole 2x2x4 slice. The times are simulated.
32 devices in a mesh: groups: 2 (over x), tm: 16 (over z, y, core).
Axes of the slice: x: 2, y: 2, z: 4, core: 2. Of those that a mesh axis runs over, the one named last changes fastest.
Arguments:
- queries: bfloat16 [12288, 2240], P(('groups', 'tm')), parts along dimension 0, may hold values from -40 to 40
- keys: bfloat16 [12288, 2240], P(('groups', 'tm')), parts along dimension 0, may hold values from -6 to 6
- values: bfloat16 [12288, 2240], P(('groups', 'tm')), parts along dimension 0, may hold values from -6 to 6
- cross_queries: bfloat16 [12288, 2240], P(('groups', 'tm')), parts along dimension 0, may hold values from -540 to 540
- prompt_keys: bfloat16 [32, 128, 2240], P(('groups', 'tm')), parts along dimension 0, may hold values from -6 to 6
- prompt_values: bfloat16 [32, 128, 2240], P(('groups', 'tm')), parts along dimension 0, may hold values from -6 to 6
- caption_keys: bfloat16 [256, 2240], P('groups'), parts along dimension 0, may hold values from -6 to 6
- caption_values: bfloat16 [256, 2240], P('groups'), parts along dimension 0, may hold values from -6 to 6
- span_start: int32 [32], P('groups'), parts along dimension 0, may hold values from 0 to 15, as said below
- span_end: int32 [32], P('groups'), parts along dimension 0, may hold values from 1 to 16
- prompt_tokens: int32 [32], P('groups'), parts along dimension 0, may hold values from 80 to 128, as said below
- region_mask: int32 [32, 3], P('groups'), parts along dimension 0, may hold values 0 or 1
- out_gain: float32 [2240], replicated, may hold values from 0.5 to 1.5
Outputs:
- self_mixed: bfloat16 [12288, 2240], P(('groups', 'tm')), parts along dimension 0
- cross_mixed: bfloat16 [12288, 2240], P(('groups', 'tm')), parts along dimension 0
There are 2 independent parts, one for each index of `groups`. A program takes and returns all parts, laid end to end along the dimension named above; an argument that names none is the same for every part. Nothing has to cross between parts.
Inputs may be any that keep to these rules, and one draw needn't show every extreme that they name: Prompt p applies to stretches span_start[p] to span_end[p] - 1, with p <= span_start[p] <= p + 1 and span_start[p] < span_end[p] <= p + 6; prompt 0 covers stretches 0 to 5. `prompt_tokens`: prompt 0 uses all 128 slots.
All inputs are finite; a program needn't handle non-finite values.
Results may differ from a plain program's by a relative error of at most 0.007.
Values may be sent and summed in bfloat16 or wider, within the bound.
No kernel may reach another device: no remote copies, remote signals or barrier semaphores. Data moves between devices by JAX's collectives and lax.ppermute only.
A program may use at most 128 MiB of HBM per device.

v0:
```python
import functools
import math

import jax
import jax.numpy as jnp
from jax import lax
from jax.experimental import pallas as pl
from jax.experimental.pallas import tpu as pltpu
from jax.sharding import PartitionSpec as P

HD = 32
SPAN = 6
QUAD = 128
LAYER = 4
BF = jnp.bfloat16
F32 = jnp.float32
EMPTY = -1e30
STEP = 3
PARTS = 3
COPIES = 2
ROOM = 66_900_000


def vmem():
    return pl.BlockSpec(memory_space=pltpu.VMEM)


def smem():
    return pl.BlockSpec(memory_space=pltpu.SMEM)


def anywhere():
    return pl.BlockSpec(memory_space=pl.ANY)


def cost(flops, moved, exps=0):
    flops, moved = flops // 1000, moved // 1000
    return pl.CostEstimate(flops=flops, bytes_accessed=moved, transcendentals=exps)


def quad_rows(ref, q, width):
    if (q + 1) * QUAD <= width:
        return ref[q * QUAD : (q + 1) * QUAD, :]
    part = ref[q * QUAD : width, :]
    fill = jnp.zeros(((q + 1) * QUAD - width, part.shape[1]), part.dtype)
    return jnp.concatenate([part, fill], axis=0)


def part_rows(width, quads, part):
    low = part * (quads // PARTS) * QUAD
    return pl.ds(low, min(quads // PARTS * QUAD, width - low))


def turned_quad(keys, used, rows):
    turned = jnp.transpose(keys.astype(F32))
    return jnp.where(rows < used, turned, turned[0:1, :]).astype(BF)


def no_kernel(*refs):
    del refs


def after(blocks, *tokens):
    return pl.pallas_call(
        no_kernel,
        in_specs=[anywhere()] * (len(blocks) + len(tokens)),
        out_specs=[anywhere()] * len(blocks),
        out_shape=[jax.ShapeDtypeStruct(block.shape, block.dtype) for block in blocks],
        input_output_aliases={place: place for place in range(len(blocks))},
        cost_estimate=cost(0, 0),
        name="after",
    )(*blocks, *tokens)


def across_kernel(waits, count, own_hbm, up_hbm, *refs):
    states_hbm, refs = refs[waits : waits + count], refs[waits + count :]
    across_hbm, _, *refs = refs
    if count:
        sent_hbm, held, in_sems, out_sems, own_state, partners, sent_here, state_sems = refs
    else:
        held, in_sems, out_sems = refs
    lower = lax.axis_index("tm") % LAYER < LAYER // 2
    piece = own_hbm.shape[0] // COPIES

    def move_in(source, part):
        at = pl.ds(part * piece, piece)
        return pltpu.make_async_copy(source.at[at], held.at[at], in_sems.at[part])

    def move_out(part):
        at = pl.ds(part * piece, piece)
        return pltpu.make_async_copy(held.at[at], across_hbm.at[at], out_sems.at[part])

    @pl.when(lower)
    def _():
        for part in range(COPIES):
            move_in(own_hbm, part).start()

    @pl.when(jnp.logical_not(lower))
    def _():
        for part in range(COPIES):
            move_in(up_hbm, part).start()

    moves = []
    for n in range(count):
        into = partners.at[n - 1] if n else own_state
        moves.append(pltpu.make_async_copy(states_hbm[n], into, state_sems.at[n]))
    for move in moves:
        move.start()
    for part in range(COPIES):
        move_in(up_hbm, part).wait()
        move_out(part).start()
    for move in moves:
        move.wait()
    if count:
        digit_step(own_state, [partners.at[n] for n in range(count - 1)], sent_here)
        away = pltpu.make_async_copy(sent_here, sent_hbm, state_sems.at[count])
        away.start()
        away.wait()
    for part in range(COPIES):
        move_out(part).wait()


def to_cross(own, up, *tokens, states=()):
    shape = jax.ShapeDtypeStruct(own.shape, own.dtype)
    outs = [shape, shape]
    scratch = [
        pltpu.VMEM(own.shape, own.dtype),
        pltpu.SemaphoreType.DMA((COPIES,)),
        pltpu.SemaphoreType.DMA((COPIES,)),
    ]
    if states:
        state = states[0].shape
        outs.append(jax.ShapeDtypeStruct(state, BF))
        scratch += [
            pltpu.VMEM(state, F32),
            pltpu.VMEM((len(states) - 1,) + state, BF),
            pltpu.VMEM(state, BF),
            pltpu.SemaphoreType.DMA((len(states) + 1,)),
        ]
    return pl.pallas_call(
        functools.partial(across_kernel, len(tokens), len(states)),
        in_specs=[anywhere()] * (2 + len(tokens) + len(states)),
        out_specs=[anywhere()] * len(outs),
        out_shape=outs,
        input_output_aliases={1: 1},
        scratch_shapes=scratch,
        cost_estimate=cost(0, 4 * own.size),
        compiler_params=pltpu.CompilerParams(vmem_limit_bytes=ROOM),
        name="to_cross",
    )(own, up, *tokens, *states)


def attend_kernel(setup, start_ref, end_ref, tokens_ref, region_ref, *refs):
    count, first, last, held, waits, prompts, width, tokens, tiles = setup
    tile = tokens // tiles
    quads = -(-width // QUAD)
    rounds = quads // STEP
    query_hbm, refs = refs[0], refs[1:]
    key_hbm, refs = refs[:count], refs[count:]
    value_hbm, refs = refs[:count], refs[count + waits :]
    if not first:
        state_in, refs = refs[:2], refs[2:]
    if last:
        out_ref, refs = refs[0], refs[1:]
    else:
        state_out, refs = refs[:2], refs[2:]
    keys, vals, marks, queries, spread, levels, totals, level, total, *refs = refs
    s_a, s_b, p_a, p_b, f_a, f_b, work, found, used, ready, sems, tile_sems = refs
    scale = math.log2(math.e) / math.sqrt(HD)
    none = jnp.zeros((HD, tile), BF)
    i = pl.program_id(0)

    def copies(b, at):
        return (
            pltpu.make_async_copy(key_hbm[b], keys.at[at], sems.at[at, 0]),
            pltpu.make_async_copy(value_hbm[b], vals.at[at, pl.ds(0, width)], sems.at[at, 1]),
        )

    def query_move(t):
        columns = pl.ds(t * tile, tile)
        return pltpu.make_async_copy(query_hbm.at[:, columns], queries.at[t], tile_sems.at[t, 0])

    def state_moves(t, into):
        for place, held_here in enumerate((levels, totals)):
            if into:
                yield pltpu.make_async_copy(state_in[place].at[t], held_here.at[t], tile_sems.at[t, 1 + place])
            else:
                yield pltpu.make_async_copy(held_here.at[t], state_out[place].at[t], tile_sems.at[t, 3 + place])

    @pl.when(i == 0)
    def _():
        if last:
            for move in state_moves(0, True):
                move.start()
        stretch = lax.axis_index("tm")
        wanted = []
        lengths = [jnp.int32(0)] * tiles
        for b, owner in enumerate(held(stretch)):
            if owner is None:
                seen = [jnp.int32(1)] * tiles
                used[b] = jnp.int32(QUAD)
            else:
                safe = jnp.clip(owner, 0, prompts - 1)
                covers = (
                    (owner >= 0)
                    & (start_ref[safe] <= stretch)
                    & (stretch < end_ref[safe])
                )
                used[b] = tokens_ref[safe]
                seen = [
                    (covers & (region_ref[t, safe] == 1)).astype(jnp.int32)
                    for t in range(tiles)
                ]
            for t in range(tiles):
                work[t * count + lengths[t]] = jnp.int32(b)
                lengths[t] = lengths[t] + seen[t]
            wanted.append(functools.reduce(jnp.add, seen) > 0)
            ready[b] = jnp.int32(0)

            @pl.when(wanted[b])
            def _():
                for move in copies(b, b):
                    move.start()

        for t in range(tiles):
            found[t] = lengths[t]

            @pl.when(lengths[t] > 0)
            def _():
                query_move(t).start()

            if not first and not (last and t == 0):

                @pl.when((lengths[t] > 0) | last)
                def _():
                    for move in state_moves(t, True):
                        move.start()

        for q in range(quads):
            for h in range(QUAD // HD):
                off = (1 - h % 2) * tile
                spread[q, h * HD : (h + 1) * HD, off : off + tile] = none
        lanes = lax.broadcasted_iota(jnp.int32, (16, QUAD), 1)
        for b in range(count):
            marks[b] = jnp.where(lanes < used[b], 1.0, 0.0).astype(BF)
            if width < quads * QUAD:
                vals[b, width:, :] = jnp.zeros((quads * QUAD - width, QUAD), BF)

    def arrived(b):
        @pl.when(ready[b] == 0)
        def _():
            for move in copies(0, b):
                move.wait()
            ready[b] = jnp.int32(1)

    low_half = lax.broadcasted_iota(jnp.int32, (QUAD, QUAD), 1) < QUAD // 2
    row16 = lax.broadcasted_iota(jnp.int32, (16, QUAD), 0)
    zeros = jnp.zeros((QUAD // 2, QUAD), BF)

    def score(b, g, s_to):
        for k in range(STEP):
            block = keys[b, g * STEP + k].astype(F32)
            both = jnp.concatenate(
                [jnp.where(low_half, block, 0.0), jnp.where(low_half, 0.0, block)], axis=0
            ).astype(BF)
            s_to[k] = jnp.dot(both, spread[g * STEP + k], preferred_element_type=F32)

    def weigh(g, s_from, p_to, f_to):
        for k in range(STEP):
            q = g * STEP + k
            for pair in range(2):
                at = slice(pair * QUAD, (pair + 1) * QUAD)
                part = s_from[k, at, :]
                old = level[q, pair : pair + 1]
                new = jnp.maximum(old, jnp.max(part, axis=0, keepdims=True))
                p_to[k, at, :] = jnp.exp2((part - new) * scale).astype(BF)
                f_to[k, pair : pair + 1] = jnp.exp2((old - new) * scale)
                level[q, pair : pair + 1] = new

    def mix(b, many, ones, g, p_from, f_from):
        for k in range(STEP):
            q = g * STEP + k
            v = vals[b, q * QUAD : (q + 1) * QUAD, :] * many
            left = jnp.concatenate(
                [
                    jnp.concatenate([v[: QUAD // 2], zeros], axis=1),
                    jnp.concatenate([zeros, v[QUAD // 2 :]], axis=1),
                    ones,
                ],
                axis=0,
            )
            out = jnp.dot(left, p_from[k], preferred_element_type=F32)
            factor = f_from[k]
            level[q, 2:4] = level[q, 2:4] * factor + out[QUAD : QUAD + 2]
            for pair in range(2):
                r = pair * 2 * HD
                added = jnp.concatenate([out[r : r + HD, :tile], out[r + HD : r + 2 * HD, tile:]], axis=1)
                at = slice(pair * HD, (pair + 1) * HD)
                total[q, at, :] = total[q, at, :] * factor[pair : pair + 1] + added

    slots = [(s_a, p_a, f_a), (s_b, p_b, f_b)]
    n = found[i]
    if first:
        level[:, 0:2] = jnp.full((quads, 2, 2 * tile), EMPTY, F32)
        level[:, 2:4] = jnp.zeros((quads, 2, 2 * tile), F32)
        total[...] = jnp.zeros(total.shape, F32)
    else:

        @pl.when((n > 0) | last)
        def _():
            for move in state_moves(i, True):
                move.wait()
            level[...] = levels[i]
            total[...] = totals[i]

    @pl.when(n > 0)
    def _():
        query_move(i).wait()
        for r in range(0, quads * QUAD, HD):
            q, h = r // QUAD, r % QUAD // HD
            on = h % 2 * tile
            piece = queries[i, r : r + HD, :] if r < width else none
            spread[q, h * HD : (h + 1) * HD, on : on + tile] = piece
        b0 = work[i * count]
        arrived(b0)
        score(b0, 0, s_a)
        weigh(0, s_a, p_a, f_a)
        score(b0, 1, s_b)

        def entry(j, carry):
            b = work[i * count + j]
            later = work[i * count + jnp.minimum(j + 1, n - 1)]
            arrived(later)
            mark = marks[b]
            many = jnp.concatenate([mark] * (QUAD // 16), axis=0)
            mark = mark.astype(F32)
            ones = jnp.concatenate(
                [jnp.where(row16 == 0, mark, 0.0), jnp.where(row16 == 1, mark, 0.0)], axis=1
            ).astype(BF)
            for g in range(rounds):
                here, there = slots[g % 2], slots[(g + 1) % 2]
                score(b if g + 2 < rounds else later, (g + 2) % rounds, here[0])
                mix(b, many, ones, g, here[1], here[2])
                weigh((g + 1) % rounds, there[0], there[1], there[2])
            return carry

        lax.fori_loop(0, n, entry, 0)

    if last:
        for q in range(quads):
            scaled = 1.0 / level[q, 2:4]
            for pair in range(2):
                mixed = total[q, pair * HD : (pair + 1) * HD, :] * scaled[pair : pair + 1]
                for side in range(2):
                    r = q * QUAD + (2 * pair + side) * HD
                    if r < width:
                        out_ref[r : r + HD, :] = mixed[:, side * tile : (side + 1) * tile].astype(BF)
    else:

        @pl.when((n > 0) | first)
        def _():
            levels[i] = level[...]
            totals[i] = total[...]
            for move in state_moves(i, False):
                move.start()

        @pl.when(i == tiles - 1)
        def _():
            for t in range(tiles):

                @pl.when((found[t] > 0) | first)
                def _():
                    for move in state_moves(t, False):
                        move.wait()


def attend(spans, queries, blocks, held, state, last, waits=()):
    width, tokens = queries.shape
    quads = -(-width // QUAD)
    count = len(blocks)
    tiles, prompts = spans[3].shape
    tile = tokens // tiles
    first = state is None
    setup = (count, first, last, held, len(waits), prompts, width, tokens, tiles)
    level, total = (quads, 4, 2 * tile), (quads, 2 * HD, 2 * tile)
    aliases = {}
    if last:
        outs = [jax.ShapeDtypeStruct((width, tokens), BF)]
        out_specs = [pl.BlockSpec((width, tile), lambda i: (0, i))]
    else:
        outs = [jax.ShapeDtypeStruct((tiles,) + shape, F32) for shape in (level, total)]
        out_specs = [anywhere()] * 2
        if not first:
            at = 5 + 2 * count + len(waits)
            aliases = {at: 0, at + 1: 1}
    keys = [block[0] for block in blocks]
    values = [block[1] for block in blocks]
    scratch = [
        pltpu.VMEM((count, quads, QUAD, QUAD), BF),
        pltpu.VMEM((count, quads * QUAD, QUAD), BF),
        pltpu.VMEM((count, 16, QUAD), BF),
        pltpu.VMEM((tiles, width, tile), BF),
        pltpu.VMEM((quads, QUAD, 2 * tile), BF),
        pltpu.VMEM((tiles,) + level, F32),
        pltpu.VMEM((tiles,) + total, F32),
        pltpu.VMEM(level, F32),
        pltpu.VMEM(total, F32),
    ]
    scratch += [pltpu.VMEM((STEP, 2 * QUAD, 2 * tile), F32)] * 2
    scratch += [pltpu.VMEM((STEP, 2 * QUAD, 2 * tile), BF)] * 2
    scratch += [pltpu.VMEM((STEP, 2, 2 * tile), F32)] * 2
    scratch += [
        pltpu.SMEM((count * tiles + 1,), jnp.int32),
        pltpu.SMEM((tiles,), jnp.int32),
        pltpu.SMEM((count,), jnp.int32),
        pltpu.SMEM((count,), jnp.int32),
        pltpu.SemaphoreType.DMA((count, 2)),
        pltpu.SemaphoreType.DMA((tiles, 5)),
    ]
    area = count * QUAD * tokens
    return pl.pallas_call(
        functools.partial(attend_kernel, setup),
        grid=(tiles,),
        in_specs=[smem()] * 4 + [anywhere()] * (1 + 2 * count + len(waits) + (0 if first else 2)),
        out_specs=out_specs,
        out_shape=outs,
        scratch_shapes=scratch,
        input_output_aliases=aliases,
        cost_estimate=cost(40 * area * width, 4 * width * tokens, area * width // HD),
        compiler_params=pltpu.CompilerParams(vmem_limit_bytes=ROOM),
        name="attend",
    )(
        *spans,
        queries,
        *keys,
        *values,
        *waits,
        *([] if first else state),
    )


def front_kernel(tokens_ref, *refs):
    sources, (own_ref, sent_ref), turned_hbm, refs = refs[:4], refs[4:6], refs[6:8], refs[8:]
    arrays, turned, (in_sems, out_sems) = refs[:4], refs[4:6], refs[6:]
    rows = lax.broadcasted_iota(jnp.int32, (QUAD, QUAD), 0)
    columns = lax.broadcasted_iota(jnp.int32, (QUAD, QUAD), 1)
    width, quads = arrays[0].shape[0], sent_ref.shape[0]
    every = quads // PARTS

    def move_in(n, part):
        at = part_rows(width, quads, part)
        return pltpu.make_async_copy(sources[n].at[at], arrays[n].at[at], in_sems.at[n, part])

    def move_out(n, part):
        at = pl.ds(part * every, every)
        return pltpu.make_async_copy(turned[n].at[at], turned_hbm[n].at[at], out_sems.at[n, part])

    for part in range(PARTS):
        for n in range(2):
            move_in(n, part).start()
    for n in range(2, 4):
        for part in range(PARTS):
            move_in(n, part).start()
    for n in range(2):
        used = QUAD if n else tokens_ref[lax.axis_index("tm")]
        for q in range(quads):
            if q % every == 0:
                move_in(2 + n, q // every).wait()
            turned[n][q] = turned_quad(quad_rows(arrays[2 + n], q, width), used, rows)
            if q % every == every - 1:
                move_out(n, q // every).start()
    for q in range(quads):
        if q % every == 0:
            for n in range(2):
                move_in(n, q // every).wait()
        lifted = jnp.maximum(quad_rows(arrays[0], q, width), 0)
        grown = lax.dot_general(
            quad_rows(arrays[1], q, width), lifted, (((1,), (1,)), ((), ())), preferred_element_type=F32
        )
        grown = jnp.where(rows // HD == columns // HD, grown, 0.0)
        folded = grown[0:HD] + grown[HD : 2 * HD] + grown[2 * HD : 3 * HD] + grown[3 * HD :]
        own_ref[q] = folded
        sent_ref[q] = folded.astype(BF)
    for n in range(2):
        for part in range(PARTS):
            move_out(n, part).wait()


def front(tokens, keys, values, prompt_keys, caption_keys):
    width = keys.shape[0]
    quads = -(-width // QUAD)
    arrays = (keys, values, prompt_keys, caption_keys)
    state, turned = (quads, HD, QUAD), (quads, QUAD, QUAD)
    return pl.pallas_call(
        front_kernel,
        in_specs=[smem()] + [anywhere()] * 4,
        out_specs=[vmem()] * 2 + [anywhere()] * 2,
        out_shape=[jax.ShapeDtypeStruct(state, F32), jax.ShapeDtypeStruct(state, BF)]
        + [jax.ShapeDtypeStruct(turned, BF)] * 2,
        scratch_shapes=[pltpu.VMEM(array.shape, BF) for array in arrays]
        + [pltpu.VMEM(turned, BF)] * 2
        + [pltpu.SemaphoreType.DMA((4, PARTS)), pltpu.SemaphoreType.DMA((2, PARTS))],
        cost_estimate=cost(8 * width * QUAD * keys.shape[1], 4 * keys.size),
        compiler_params=pltpu.CompilerParams(vmem_limit_bytes=ROOM),
        name="front",
    )(tokens, *arrays)


def lower_sum(hop, prior, partners):
    digit = lax.axis_index("tm") // hop % (len(partners) + 1)
    for d, partner in enumerate(partners, 1):
        prior = prior + jnp.where((digit ^ d) < digit, partner.astype(F32), 0.0)
    return prior


def digit_step(own_ref, partners, sent_out):
    for q in range(sent_out.shape[0]):
        whole = own_ref[q]
        for partner in partners:
            whole = whole + partner[q].astype(F32)
        sent_out[q] = whole.astype(BF)


def digit_kernel(own_ref, *refs):
    digit_step(own_ref, refs[:-2], refs[-1])


def digit_sums(own, partners, token):
    return pl.pallas_call(
        digit_kernel,
        in_specs=[vmem()] * (1 + len(partners)) + [anywhere()],
        out_specs=vmem(),
        out_shape=jax.ShapeDtypeStruct(own.shape, BF),
        cost_estimate=cost(0, 8 * own.size),
        compiler_params=pltpu.CompilerParams(vmem_limit_bytes=ROOM),
        name="digit_sums",
    )(own, *partners, token)


def digits_of(size):
    hop, digits = 1, []
    while hop < size:
        radix = LAYER if hop == 1 and size % LAYER == 0 else 2
        digits.append((hop, radix))
        hop *= radix
    return digits


def swapped(block, hop, radix):
    size = lax.axis_size("tm")
    return [sent(block, [(i, i ^ (d * hop)) for i in range(size)]) for d in range(1, radix)]


def norm_kernel(digits, queries_hbm, gain_hbm, own_hbm, *refs):
    count = sum(radix - 1 for _, radix in digits)
    partners_hbm, refs = refs[:count], refs[count + 1 :]
    out_hbm, queries, raw, out, gain_ref, own_ref, partners, in_sems, out_sems, state_sems = refs
    rows = lax.broadcasted_iota(jnp.int32, (QUAD, QUAD), 0) // HD
    columns = lax.broadcasted_iota(jnp.int32, (QUAD, QUAD), 1) // HD
    width = queries.shape[0]
    quads, tokens = raw.shape[0], raw.shape[2]
    every = quads // PARTS

    def move_in(part):
        at = part_rows(width, quads, part)
        return pltpu.make_async_copy(queries_hbm.at[at], queries.at[at], in_sems.at[part])

    def move_out(part):
        at = part_rows(width, quads, part)
        return pltpu.make_async_copy(out.at[at], out_hbm.at[at], out_sems.at[part])

    moves = [
        pltpu.make_async_copy(own_hbm, own_ref, state_sems.at[count]),
        pltpu.make_async_copy(gain_hbm, gain_ref, state_sems.at[count + 1]),
    ]
    for n in range(count):
        moves.append(pltpu.make_async_copy(partners_hbm[n], partners.at[n], state_sems.at[n]))
    for move in moves:
        move.start()
    for part in range(PARTS):
        move_in(part).start()
    for move in moves:
        move.wait()
    squares = jnp.zeros((1, tokens), F32)
    for q in range(quads):
        if q % every == 0:
            move_in(q // every).wait()
        whole, first = own_ref[q], 0
        for hop, radix in digits:
            whole = lower_sum(hop, whole, [partners[first + n, q] for n in range(radix - 1)])
            first += radix - 1
        whole = whole.astype(BF).astype(F32)
        wide = jnp.where(rows == columns, jnp.concatenate([whole] * (QUAD // HD), axis=0), 0.0).astype(BF)
        lifted = jnp.maximum(quad_rows(queries, q, width), 0)
        part = jnp.dot(wide, lifted, preferred_element_type=F32)
        raw[q] = part
        squares = squares + jnp.sum(part * part, axis=0, keepdims=True)
    factor = lax.rsqrt(squares / width + 1e-05)
    for q in range(quads):
        size = min(QUAD, width - q * QUAD)
        gain = gain_ref[:, q * QUAD : q * QUAD + size]
        if size < QUAD:
            gain = jnp.concatenate([gain, jnp.zeros((1, QUAD - size), F32)], axis=1)
        gains = jnp.transpose(jnp.broadcast_to(gain, (QUAD, QUAD)))
        gains = jnp.concatenate([gains] * (tokens // QUAD), axis=1)
        mixed = (raw[q] * factor * gains).astype(BF)
        out[q * QUAD : q * QUAD + size, :] = mixed[:size]
        if q % every == every - 1:
            move_out(q // every).start()
    for part in range(PARTS):
        move_out(part).wait()


def self_mix(queries, own, gain, partners, digits, token):
    width, tokens = queries.shape
    quads = -(-width // QUAD)
    return pl.pallas_call(
        functools.partial(norm_kernel, tuple(digits)),
        in_specs=[anywhere()] * (4 + len(partners)),
        out_specs=anywhere(),
        out_shape=jax.ShapeDtypeStruct((width, tokens), BF),
        scratch_shapes=[
            pltpu.VMEM((width, tokens), BF),
            pltpu.VMEM((quads, QUAD, tokens), F32),
            pltpu.VMEM((width, tokens), BF),
            pltpu.VMEM(gain.shape, F32),
            pltpu.VMEM(own.shape, F32),
            pltpu.VMEM((len(partners),) + own.shape, BF),
            pltpu.SemaphoreType.DMA((PARTS,)),
            pltpu.SemaphoreType.DMA((PARTS,)),
            pltpu.SemaphoreType.DMA((len(partners) + 2,)),
        ],
        cost_estimate=cost(8 * width * QUAD * tokens, 4 * width * tokens),
        compiler_params=pltpu.CompilerParams(vmem_limit_bytes=ROOM),
        name="self_mix",
    )(queries, gain, own, *partners, token)


def sent(block, pairs):
    return lax.ppermute(block, "tm", pairs)


def local(
    queries,
    keys,
    values,
    cross_queries,
    prompt_keys,
    prompt_values,
    caption_keys,
    caption_values,
    span_start,
    span_end,
    prompt_tokens,
    region_mask,
    out_gain,
):
    size = lax.axis_size("tm")
    slots, width = prompt_keys.shape[1:]
    spans = (span_start, span_end, prompt_tokens, jnp.transpose(region_mask))
    turned = lambda block: jnp.transpose(block.reshape(slots, width))
    queries_t = jnp.transpose(cross_queries)
    call = functools.partial(attend, spans, queries_t)

    bases = [LAYER * z for z in range(size // LAYER)]
    beside = [(i, i ^ 1) for i in range(size)]
    up = [(i, (i + LAYER) % size) for i in range(size)]
    swap = [(i, i ^ 2) for i in range(size)]
    onward = [(i, i + LAYER - 1) for i in range(size) if i % 2 and i + LAYER - 1 < size]
    further = [(i, i + 1) for i in range(size) if i % 2 and i + 1 < size]
    spot = lambda c: c % LAYER
    pick = lambda c, *ways: functools.reduce(
        lambda rest, way: jnp.where(spot(c) == way[0], c - way[1], rest), ways, -1
    )
    digits = digits_of(size)

    own_v = turned(prompt_values)
    up_v = sent(own_v, up)
    own_v_beside = sent(own_v, beside)
    own_sums, going, own_k, caption_k = front(
        prompt_tokens,
        jnp.transpose(keys),
        jnp.transpose(values),
        turned(prompt_keys),
        jnp.transpose(caption_keys),
    )
    partners = swapped(going, *digits[0])
    gain_row = out_gain.reshape(1, width)
    state = call([(caption_k, jnp.transpose(caption_values))], lambda c: [None], None, False, waits=[going])

    summed = [own_sums, *partners] if len(digits) > 2 else []
    across_v, up_v, *going = to_cross(own_v, up_v, state[0], own_v_beside, *partners, states=summed)
    swap_v = sent(across_v, swap)
    (late_k,) = after([own_k], state[0])
    up_k = sent(late_k, up)
    own_k_beside = sent(late_k, beside)
    up_v_beside = sent(up_v, beside)
    for place, digit in enumerate(digits[1:-1]):
        if place:
            going = [digit_sums(own_sums, partners, across_v)]
        partners += swapped(going[0], *digit)
    state = call(
        [(late_k, own_v), (own_k_beside, own_v_beside)],
        lambda c: [c, pick(c, (1, 1), (3, 1))],
        state,
        False,
        waits=[across_v, gain_row],
    )

    (swap_v,) = after([swap_v], state[0])
    summed = [own_sums, *partners] if len(digits) > 1 else []
    across_k, up_k, *going = to_cross(late_k, up_k, state[0], up_v_beside, *partners, states=summed)
    swap_k = sent(across_k, swap)
    far_k = sent(up_k, further)
    far_v = sent(swap_v, onward)
    up_k_beside = sent(up_k, beside)
    final = swapped(going[0], *digits[-1]) if len(digits) > 1 else []
    state = call(
        [(up_k, up_v), (up_k_beside, up_v_beside)],
        lambda c: [c - LAYER, pick(c, (0, 3), (2, 3), (1, 5), (3, 5))],
        state,
        False,
        waits=[across_k],
    )

    swap_k, swap_v = after([swap_k, swap_v], state[0], far_v, *final)
    swap_k_beside = sent(swap_k, beside)
    swap_v_beside = sent(swap_v, beside)
    self_mixed = self_mix(jnp.transpose(queries), own_sums, gain_row, partners + final, digits, swap_k)
    cross_mixed = call(
        [(swap_k, swap_v), (swap_k_beside, swap_v_beside), (far_k, far_v)],
        lambda c: [
            c - 2,
            pick(c, (0, 1), (1, 3), (2, 1), (3, 3)),
            pick(c, (0, 5), (2, 5)),
        ],
        state,
        True,
        waits=[self_mixed],
    )[0]
    return (jnp.transpose(self_mixed), jnp.transpose(cross_mixed))


def solution(mesh):
    in_specs = (
        P(("groups", "tm"), None),
        P(("groups", "tm"), None),
        P(("groups", "tm"), None),
        P(("groups", "tm"), None),
        P(("groups", "tm"), None, None),
        P(("groups", "tm"), None, None),
        P("groups", None),
        P("groups", None),
        P("groups"),
        P("groups"),
        P("groups"),
        P("groups", None),
        P(),
    )
    out_specs = (P(("groups", "tm"), None), P(("groups", "tm"), None))
    return jax.shard_map(local, mesh=mesh, in_specs=in_specs, out_specs=out_specs, check_vma=False)
```

profile of v0, /device:TPU:16, one launch (start us, length us, event | category | flops | bytes accessed | tf_op | source)
XLA Modules:
  0.0 81.4 jit_solution(14766697459834420159)
XLA Ops:
  0.6 0.1 collective-permute-start.4
  0.7 1.6 %collective-permute-start.3 = (bf16[2240,128]{1,0:T(8,128)(2,1)}, bf16[2240,128]{1,0:T(8,128)(2,1)}, u32[]{:S(2)}, u32[]{:S(2)}) collective-permute-start(bf16[2240,128]{1,0:T(8,128)(2,1)} %bitcast.22), channel_id=1, source_target_pairs={{0,4},{1,5},{2,6},{3,7},{4,8},{5,9},{6,10},{7,11},{8,12},{9,13},{1... | collective-permute-start | bytes 1720328 | tf_op jit(solution)/shard_map/ppermute | solution.py:640
  2.3 5.6 %front.1 = (f32[18,32,128]{2,1,0:T(8,128)}, bf16[18,32,128]{2,1,0:T(8,128)(2,1)}, bf16[18,128,128]{2,1,0:T(8,128)(2,1)}, bf16[18,128,128]{2,1,0:T(8,128)(2,1)}) custom-call(s32[16]{0:T(128)} %tokens_ref.9, bf16[2240,384]{1,0:T(8,128)(2,1)} %bitcast.15, bf16[2240,384]{1,0:T(8,128)(2,1)} %bitcast.16, bf16[2240,128]{1,0:T(8,128)(2,1)} %bitcast.19, ...), custom_call_target="tpu_custom_call" | custom-call | flops 880803 | bytes 3440 | tf_op jit(solution)/shard_map/front/pallas_call | solution.py:494
  7.9 0.2 collective-permute-start
  8.1 1.5 %collective-permute-start.1 = (bf16[18,32,128]{2,1,0:T(8,128)(2,1)}, bf16[18,32,128]{2,1,0:T(8,128)(2,1)}, u32[]{:S(2)}, u32[]{:S(2)}) collective-permute-start(bf16[18,32,128]{2,1,0:T(8,128)(2,1)} %get-tuple-element.21.refs_3_), channel_id=1, source_target_pairs={{0,2},{1,3},{2,0},{3,1},{4,6},{5,7},{6,4},{7,5},{8,10},{9,11},{10,... | collective-permute-start | bytes 442376 | tf_op jit(solution)/shard_map/ppermute | solution.py:640
  9.7 0.2 collective-permute-start.2
  9.8 9.2 %attend.4 = (f32[3,18,4,256]{3,2,1,0:T(4,128)}, f32[3,18,64,256]{3,2,1,0:T(8,128)}) custom-call(s32[16]{0:T(128)} %start_ref.7, s32[16]{0:T(128)} %end_ref.7, s32[16]{0:T(128)} %tokens_ref.9, s32[3,16]{1,0:T(4,128)} %bitcast.30, bf16[2240,384]{1,0:T(8,128)(2,1)} %bitcast.25, bf16[18,128,128]{2,1,0:T(8,128)(2,1)} %get-tuple-element.22.refs_1_, ...), custom_call_target="tpu_custom_call" | custom-call | flops 4404019 | bytes 3440 | tf_op jit(solution)/shard_map/attend/pallas_call | solution.py:421
  19.1 0.0 copy-start
  19.1 0.0 collective-permute-done.refs_2_.refs_6_.refs_7_.refs_0_
  19.1 0.5 collective-permute-start.7
  19.6 0.0 collective-permute-done.1.refs_3_.refs_7_.refs_8_.refs_1_
  19.6 0.3 collective-permute-start.6
  19.9 0.0 collective-permute-done.2.refs_4_.refs_8_.refs_9_.refs_2_
  19.9 0.0 collective-permute-done.4.refs_1_.refs_4_
  19.9 0.0 collective-permute-done.3.up_hbm
  19.9 2.2 %to_cross.2 = (bf16[2240,128]{1,0:T(8,128)(2,1)}, bf16[2240,128]{1,0:T(8,128)(2,1)}, bf16[18,32,128]{2,1,0:T(8,128)(2,1)}) custom-call(bf16[2240,128]{1,0:T(8,128)(2,1)} %bitcast.23, bf16[2240,128]{1,0:T(8,128)(2,1)} %collective-permute-done.3.up_hbm, f32[3,18,4,256]{3,2,1,0:T(4,128)} %get-tuple-element.23.refs_0_.refs_1_.refs_7_, ...), custom_call_target="tpu_custom_call", output_to_operand_aliasing={{1}: (1, {})} | custom-call | bytes 1146 | tf_op jit(solution)/shard_map/to_cross/pallas_call | solution.py:140
  22.1 0.1 collective-permute-start.8
  22.2 1.6 %collective-permute-start.11 = (bf16[2240,128]{1,0:T(8,128)(2,1)}, bf16[2240,128]{1,0:T(8,128)(2,1)}, u32[]{:S(2)}, u32[]{:S(2)}) collective-permute-start(bf16[2240,128]{1,0:T(8,128)(2,1)} %get-tuple-element.26.refs_5_), channel_id=1, source_target_pairs={{0,2},{1,3},{2,0},{3,1},{4,6},{5,7},{6,4},{7,5},{8,10},{9,11},{10,... | collective-permute-start | bytes 1720328 | tf_op jit(solution)/shard_map/ppermute | solution.py:640
  23.8 1.5 %collective-permute-start.5 = (bf16[18,32,128]{2,1,0:T(8,128)(2,1)}, bf16[18,32,128]{2,1,0:T(8,128)(2,1)}, u32[]{:S(2)}, u32[]{:S(2)}) collective-permute-start(bf16[18,32,128]{2,1,0:T(8,128)(2,1)} %get-tuple-element.24), channel_id=1, source_target_pairs={{0,4},{1,5},{2,6},{3,7},{4,0},{5,1},{6,2},{7,3},{8,12},{9,13},{10,... | collective-permute-start | bytes 442376 | tf_op jit(solution)/shard_map/ppermute | solution.py:640
  25.3 0.0 copy-done
  25.3 0.6 reshape.13.refs_6_.gain_hbm
  25.9 0.0 collective-permute-done.7.refs_2_
  25.9 1.1 %attend.5 = (f32[3,18,4,256]{3,2,1,0:T(4,128)}, f32[3,18,64,256]{3,2,1,0:T(8,128)}) custom-call(s32[16]{0:T(128)} %start_ref.7, s32[16]{0:T(128)} %end_ref.7, s32[16]{0:T(128)} %tokens_ref.9, s32[3,16]{1,0:T(4,128)} %bitcast.31, bf16[2240,384]{1,0:T(8,128)(2,1)} %bitcast.26, ...), custom_call_target="tpu_custom_call", output_to_operand_aliasing={{0}: (11, {}), {1}: (12, {})} | custom-call | flops 8808038 | bytes 3440 | tf_op jit(solution)/shard_map/attend/pallas_call | solution.py:421
  27.0 8.2 %collective-permute-done.6.up_hbm = bf16[18,128,128]{2,1,0:T(8,128)(2,1)} collective-permute-done((bf16[18,128,128]{2,1,0:T(8,128)(2,1)}, bf16[18,128,128]{2,1,0:T(8,128)(2,1)}, u32[]{:S(2)}, u32[]{:S(2)}) %collective-permute-start.6) | collective-permute-done | bytes 589856 | tf_op jit(solution)/shard_map/ppermute | solution.py:640
  35.2 2.9 %collective-permute-done.5.refs_5_.refs_10_.refs_3_ = bf16[18,32,128]{2,1,0:T(8,128)(2,1)} collective-permute-done((bf16[18,32,128]{2,1,0:T(8,128)(2,1)}, bf16[18,32,128]{2,1,0:T(8,128)(2,1)}, u32[]{:S(2)}, u32[]{:S(2)}) %collective-permute-start.5) | collective-permute-done | bytes 147488 | tf_op jit(solution)/shard_map/ppermute | solution.py:640
  38.2 0.0 collective-permute-done.8.refs_1_.refs_4_
  38.2 2.2 %to_cross.3 = (bf16[18,128,128]{2,1,0:T(8,128)(2,1)}, bf16[18,128,128]{2,1,0:T(8,128)(2,1)}, bf16[18,32,128]{2,1,0:T(8,128)(2,1)}) custom-call(bf16[18,128,128]{2,1,0:T(8,128)(2,1)} %after.3.refs_1_.own_hbm, bf16[18,128,128]{2,1,0:T(8,128)(2,1)} %collective-permute-done.6.up_hbm, ...), custom_call_target="tpu_custom_call", output_to_operand_aliasing={{1}: (1, {})} | custom-call | bytes 1179 | tf_op jit(solution)/shard_map/to_cross/pallas_call | solution.py:140
  40.4 0.1 collective-permute-start.12
  40.5 1.6 %collective-permute-start.10 = (bf16[18,128,128]{2,1,0:T(8,128)(2,1)}, bf16[18,128,128]{2,1,0:T(8,128)(2,1)}, u32[]{:S(2)}, u32[]{:S(2)}) collective-permute-start(bf16[18,128,128]{2,1,0:T(8,128)(2,1)} %get-tuple-element.31.refs_5_), channel_id=1, source_target_pairs={{0,2},{1,3},{2,0},{3,1},{4,6},{5,7},{6,4},{7,5},{8,10},{9,11},{10,... | collective-permute-start | bytes 1769480 | tf_op jit(solution)/shard_map/ppermute | solution.py:640
  42.0 0.0 collective-permute-done.11.refs_0_
  42.0 1.3 %collective-permute-start.13 = (bf16[2240,128]{1,0:T(8,128)(2,1)}, bf16[2240,128]{1,0:T(8,128)(2,1)}, u32[]{:S(2)}, u32[]{:S(2)}) collective-permute-start(bf16[2240,128]{1,0:T(8,128)(2,1)} %after.4.refs_1_), channel_id=1, source_target_pairs={{1,4},{3,6},{5,8},{7,10},{9,12},{11,14},{17,20},{19,22},{21,24},{2... | collective-permute-start | bytes 1720328 | tf_op jit(solution)/shard_map/ppermute | solution.py:640
  43.3 2.5 %collective-permute-start.9 = (bf16[18,32,128]{2,1,0:T(8,128)(2,1)}, bf16[18,32,128]{2,1,0:T(8,128)(2,1)}, u32[]{:S(2)}, u32[]{:S(2)}) collective-permute-start(bf16[18,32,128]{2,1,0:T(8,128)(2,1)} %get-tuple-element.30), channel_id=1, source_target_pairs={{0,8},{1,9},{2,10},{3,11},{4,12},{5,13},{6,14},{7,15},{8,0},{9,1},... | collective-permute-start | bytes 442376 | tf_op jit(solution)/shard_map/ppermute | solution.py:640
  45.9 1.5 %collective-permute-start.15 = (bf16[18,128,128]{2,1,0:T(8,128)(2,1)}, bf16[18,128,128]{2,1,0:T(8,128)(2,1)}, u32[]{:S(2)}, u32[]{:S(2)}) collective-permute-start(bf16[18,128,128]{2,1,0:T(8,128)(2,1)} %get-tuple-element.32.refs_1_), channel_id=1, source_target_pairs={{1,2},{3,4},{5,6},{7,8},{9,10},{11,12},{13,14},{17,18},{19,20},{21... | collective-permute-start | bytes 1769480 | tf_op jit(solution)/shard_map/ppermute | solution.py:640
  47.3 0.0 collective-permute-done.12.refs_2_
  47.4 12.2 %attend.6 = (f32[3,18,4,256]{3,2,1,0:T(4,128)}, f32[3,18,64,256]{3,2,1,0:T(8,128)}) custom-call(s32[16]{0:T(128)} %start_ref.7, s32[16]{0:T(128)} %end_ref.7, s32[16]{0:T(128)} %tokens_ref.9, s32[3,16]{1,0:T(4,128)} %bitcast.32, bf16[2240,384]{1,0:T(8,128)(2,1)} %bitcast.27, ...), custom_call_target="tpu_custom_call", output_to_operand_aliasing={{0}: (10, {}), {1}: (11, {})} | custom-call | flops 8808038 | bytes 3440 | tf_op jit(solution)/shard_map/attend/pallas_call | solution.py:421
  59.5 0.0 collective-permute-done.9.refs_4_
  59.5 0.0 collective-permute-done.13.refs_3_.refs_6_
  59.6 0.0 collective-permute-done.10.refs_0_
  59.6 0.1 collective-permute-start.14
  59.7 0.5 collective-permute-start.16
  60.2 4.5 %self_mix.1.refs_7_ = bf16[2240,384]{1,0:T(8,128)(2,1)} custom-call(bf16[2240,384]{1,0:T(8,128)(2,1)} %bitcast.17, f32[1,2240]{1,0:T(1,128)} %reshape.13.refs_6_.gain_hbm, f32[18,32,128]{2,1,0:T(8,128)} %get-tuple-element.20.refs_5_.refs_6_.own_hbm, bf16[18,32,128]{2,1,0:T(8,128)(2,1)} %collective-permute-done.refs_2_.refs_6_.refs_7_.refs_0_, ...), custom_call_target="tpu_custom_call" | custom-call | flops 880803 | bytes 3440 | tf_op jit(solution)/shard_map/self_mix/pallas_call | solution.py:617
  64.7 1.3 %collective-permute-done.15.refs_3_ = bf16[18,128,128]{2,1,0:T(8,128)(2,1)} collective-permute-done((bf16[18,128,128]{2,1,0:T(8,128)(2,1)}, bf16[18,128,128]{2,1,0:T(8,128)(2,1)}, u32[]{:S(2)}, u32[]{:S(2)}) %collective-permute-start.15) | collective-permute-done | bytes 589856 | tf_op jit(solution)/shard_map/ppermute | solution.py:640
  66.0 0.0 collective-permute-done.16.refs_5_
  66.0 0.0 collective-permute-done.14.refs_2_
  66.0 15.2 %attend.7 = bf16[2240,384]{1,0:T(8,128)(2,1)} custom-call(s32[16]{0:T(128)} %start_ref.7, s32[16]{0:T(128)} %end_ref.7, s32[16]{0:T(128)} %tokens_ref.9, s32[3,16]{1,0:T(4,128)} %bitcast.33, bf16[2240,384]{1,0:T(8,128)(2,1)} %bitcast.28, bf16[18,128,128]{2,1,0:T(8,128)(2,1)} %get-tuple-element.35.refs_5_.refs_1_, ...), custom_call_target="tpu_custom_call" | custom-call | flops 13212057 | bytes 3440 | tf_op jit(solution)/shard_map/attend/pallas_call | solution.py:421
  (3 shorter events, 0.0 us)
Async XLA Ops:
  0.6 19.3 %collective-permute-start.4 = (bf16[2240,128]{1,0:T(8,128)(2,1)}, bf16[2240,128]{1,0:T(8,128)(2,1)}, u32[]{:S(2)}, u32[]{:S(2)}) collective-permute-start(bf16[2240,128]{1,0:T(8,128)(2,1)} %bitcast.21), channel_id=1, source_target_pairs={{0,1},{1,0},{2,3},{3,2},{4,5},{5,4},{6,7},{7,6},{8,9},{9,8},{10,11... | collective-permute-start | bytes 1720328 | tf_op jit(solution)/shard_map/ppermute | solution.py:640
  0.7 19.2 %collective-permute-start.3 = (bf16[2240,128]{1,0:T(8,128)(2,1)}, bf16[2240,128]{1,0:T(8,128)(2,1)}, u32[]{:S(2)}, u32[]{:S(2)}) collective-permute-start(bf16[2240,128]{1,0:T(8,128)(2,1)} %bitcast.22), channel_id=1, source_target_pairs={{0,4},{1,5},{2,6},{3,7},{4,8},{5,9},{6,10},{7,11},{8,12},{9,13},{1... | collective-permute-start | bytes 1720328 | tf_op jit(solution)/shard_map/ppermute | solution.py:640
  7.9 11.2 %collective-permute-start = (bf16[18,32,128]{2,1,0:T(8,128)(2,1)}, bf16[18,32,128]{2,1,0:T(8,128)(2,1)}, u32[]{:S(2)}, u32[]{:S(2)}) collective-permute-start(bf16[18,32,128]{2,1,0:T(8,128)(2,1)} %get-tuple-element.21.refs_3_), channel_id=1, source_target_pairs={{0,1},{1,0},{2,3},{3,2},{4,5},{5,4},{6,7},{7,6},{8,9},{9,8},{10,11... | collective-permute-start | bytes 442376 | tf_op jit(solution)/shard_map/ppermute | solution.py:640
  8.1 11.5 %collective-permute-start.1 = (bf16[18,32,128]{2,1,0:T(8,128)(2,1)}, bf16[18,32,128]{2,1,0:T(8,128)(2,1)}, u32[]{:S(2)}, u32[]{:S(2)}) collective-permute-start(bf16[18,32,128]{2,1,0:T(8,128)(2,1)} %get-tuple-element.21.refs_3_), channel_id=1, source_target_pairs={{0,2},{1,3},{2,0},{3,1},{4,6},{5,7},{6,4},{7,5},{8,10},{9,11},{10,... | collective-permute-start | bytes 442376 | tf_op jit(solution)/shard_map/ppermute | solution.py:640
  9.7 10.2 %collective-permute-start.2 = (bf16[18,32,128]{2,1,0:T(8,128)(2,1)}, bf16[18,32,128]{2,1,0:T(8,128)(2,1)}, u32[]{:S(2)}, u32[]{:S(2)}) collective-permute-start(bf16[18,32,128]{2,1,0:T(8,128)(2,1)} %get-tuple-element.21.refs_3_), channel_id=1, source_target_pairs={{0,3},{1,2},{2,1},{3,0},{4,7},{5,6},{6,5},{7,4},{8,11},{9,10},{10,... | collective-permute-start | bytes 442376 | tf_op jit(solution)/shard_map/ppermute | solution.py:640
  19.1 6.2 %copy-start = (f32[2240]{0:T(1024)S(1)}, f32[2240]{0:T(1024)}, u32[]{:S(2)}) copy-start(f32[2240]{0:T(1024)} %param.25) | copy-start | bytes 26884
  19.1 6.8 %collective-permute-start.7 = (bf16[18,128,128]{2,1,0:T(8,128)(2,1)}, bf16[18,128,128]{2,1,0:T(8,128)(2,1)}, u32[]{:S(2)}, u32[]{:S(2)}) collective-permute-start(bf16[18,128,128]{2,1,0:T(8,128)(2,1)} %after.3.refs_1_.own_hbm), channel_id=1, source_target_pairs={{0,1},{1,0},{2,3},{3,2},{4,5},{5,4},{6,7},{7,6},{8,9},{9,8},{10,11... | collective-permute-start | bytes 1769480 | tf_op jit(solution)/shard_map/ppermute | solution.py:640
  19.6 15.6 %collective-permute-start.6 = (bf16[18,128,128]{2,1,0:T(8,128)(2,1)}, bf16[18,128,128]{2,1,0:T(8,128)(2,1)}, u32[]{:S(2)}, u32[]{:S(2)}) collective-permute-start(bf16[18,128,128]{2,1,0:T(8,128)(2,1)} %after.3.refs_1_.own_hbm), channel_id=1, source_target_pairs={{0,4},{1,5},{2,6},{3,7},{4,8},{5,9},{6,10},{7,11},{8,12},{9,13},{1... | collective-permute-start | bytes 1769480 | tf_op jit(solution)/shard_map/ppermute | solution.py:640
  22.1 16.1 %collective-permute-start.8 = (bf16[2240,128]{1,0:T(8,128)(2,1)}, bf16[2240,128]{1,0:T(8,128)(2,1)}, u32[]{:S(2)}, u32[]{:S(2)}) collective-permute-start(bf16[2240,128]{1,0:T(8,128)(2,1)} %get-tuple-element.29.refs_3_), channel_id=1, source_target_pairs={{0,1},{1,0},{2,3},{3,2},{4,5},{5,4},{6,7},{7,6},{8,9},{9,8},{10,11... | collective-permute-start | bytes 1720328 | tf_op jit(solution)/shard_map/ppermute | solution.py:640
  22.2 19.9 %collective-permute-start.11 = (bf16[2240,128]{1,0:T(8,128)(2,1)}, bf16[2240,128]{1,0:T(8,128)(2,1)}, u32[]{:S(2)}, u32[]{:S(2)}) collective-permute-start(bf16[2240,128]{1,0:T(8,128)(2,1)} %get-tuple-element.26.refs_5_), channel_id=1, source_target_pairs={{0,2},{1,3},{2,0},{3,1},{4,6},{5,7},{6,4},{7,5},{8,10},{9,11},{10,... | collective-permute-start | bytes 1720328 | tf_op jit(solution)/shard_map/ppermute | solution.py:640
  23.8 14.4 %collective-permute-start.5 = (bf16[18,32,128]{2,1,0:T(8,128)(2,1)}, bf16[18,32,128]{2,1,0:T(8,128)(2,1)}, u32[]{:S(2)}, u32[]{:S(2)}) collective-permute-start(bf16[18,32,128]{2,1,0:T(8,128)(2,1)} %get-tuple-element.24), channel_id=1, source_target_pairs={{0,4},{1,5},{2,6},{3,7},{4,0},{5,1},{6,2},{7,3},{8,12},{9,13},{10,... | collective-permute-start | bytes 442376 | tf_op jit(solution)/shard_map/ppermute | solution.py:640
  40.4 7.0 %collective-permute-start.12 = (bf16[18,128,128]{2,1,0:T(8,128)(2,1)}, bf16[18,128,128]{2,1,0:T(8,128)(2,1)}, u32[]{:S(2)}, u32[]{:S(2)}) collective-permute-start(bf16[18,128,128]{2,1,0:T(8,128)(2,1)} %get-tuple-element.32.refs_1_), channel_id=1, source_target_pairs={{0,1},{1,0},{2,3},{3,2},{4,5},{5,4},{6,7},{7,6},{8,9},{9,8},{10,11... | collective-permute-start | bytes 1769480 | tf_op jit(solution)/shard_map/ppermute | solution.py:640
  40.5 19.1 %collective-permute-start.10 = (bf16[18,128,128]{2,1,0:T(8,128)(2,1)}, bf16[18,128,128]{2,1,0:T(8,128)(2,1)}, u32[]{:S(2)}, u32[]{:S(2)}) collective-permute-start(bf16[18,128,128]{2,1,0:T(8,128)(2,1)} %get-tuple-element.31.refs_5_), channel_id=1, source_target_pairs={{0,2},{1,3},{2,0},{3,1},{4,6},{5,7},{6,4},{7,5},{8,10},{9,11},{10,... | collective-permute-start | bytes 1769480 | tf_op jit(solution)/shard_map/ppermute | solution.py:640
  42.0 17.5 %collective-permute-start.13 = (bf16[2240,128]{1,0:T(8,128)(2,1)}, bf16[2240,128]{1,0:T(8,128)(2,1)}, u32[]{:S(2)}, u32[]{:S(2)}) collective-permute-start(bf16[2240,128]{1,0:T(8,128)(2,1)} %after.4.refs_1_), channel_id=1, source_target_pairs={{1,4},{3,6},{5,8},{7,10},{9,12},{11,14},{17,20},{19,22},{21,24},{2... | collective-permute-start | bytes 1720328 | tf_op jit(solution)/shard_map/ppermute | solution.py:640
  43.3 16.2 %collective-permute-start.9 = (bf16[18,32,128]{2,1,0:T(8,128)(2,1)}, bf16[18,32,128]{2,1,0:T(8,128)(2,1)}, u32[]{:S(2)}, u32[]{:S(2)}) collective-permute-start(bf16[18,32,128]{2,1,0:T(8,128)(2,1)} %get-tuple-element.30), channel_id=1, source_target_pairs={{0,8},{1,9},{2,10},{3,11},{4,12},{5,13},{6,14},{7,15},{8,0},{9,1},... | collective-permute-start | bytes 442376 | tf_op jit(solution)/shard_map/ppermute | solution.py:640
  45.9 20.1 %collective-permute-start.15 = (bf16[18,128,128]{2,1,0:T(8,128)(2,1)}, bf16[18,128,128]{2,1,0:T(8,128)(2,1)}, u32[]{:S(2)}, u32[]{:S(2)}) collective-permute-start(bf16[18,128,128]{2,1,0:T(8,128)(2,1)} %get-tuple-element.32.refs_1_), channel_id=1, source_target_pairs={{1,2},{3,4},{5,6},{7,8},{9,10},{11,12},{13,14},{17,18},{19,20},{21... | collective-permute-start | bytes 1769480 | tf_op jit(solution)/shard_map/ppermute | solution.py:640
  59.6 6.4 %collective-permute-start.14 = (bf16[18,128,128]{2,1,0:T(8,128)(2,1)}, bf16[18,128,128]{2,1,0:T(8,128)(2,1)}, u32[]{:S(2)}, u32[]{:S(2)}) collective-permute-start(bf16[18,128,128]{2,1,0:T(8,128)(2,1)} %get-tuple-element.35.refs_5_.refs_1_), channel_id=1, source_target_pairs={{0,1},{1,0},{2,3},{3,2},{4,5},{5,4},{6,7},{7,6},{8,9},{9,8},{10,11... | collective-permute-start | bytes 1769480 | tf_op jit(solution)/shard_map/ppermute | solution.py:640
  59.7 6.3 %collective-permute-start.16 = (bf16[2240,128]{1,0:T(8,128)(2,1)}, bf16[2240,128]{1,0:T(8,128)(2,1)}, u32[]{:S(2)}, u32[]{:S(2)}) collective-permute-start(bf16[2240,128]{1,0:T(8,128)(2,1)} %get-tuple-element.36.refs_4_), channel_id=1, source_target_pairs={{0,1},{1,0},{2,3},{3,2},{4,5},{5,4},{6,7},{7,6},{8,9},{9,8},{10,11... | collective-permute-start | bytes 1720328 | tf_op jit(solution)/shard_map/ppermute | solution.py:640
where the time goes:
time: 80.4 us; the launch traced here: 81.4 us
  Pallas kernels  52.2 us (65%)
  starting transfers between devices  15.1 us (19%)
  waiting for transfers between devices  12.5 us (16%)
  between operations  0.97 us (1%)
    pallas_call x4, Pallas kernels, attend(): pl.pallas_call(functools.partial(attend_kernel, setup), grid=(tiles,), in...  37.8 us
    ppermute x17, starting transfers between devices, sent(): return lax.ppermute(block, 'tm', pairs)  15.1 us
    ppermute x17, waiting for transfers between devices, sent(): return lax.ppermute(block, 'tm', pairs)  12.5 us
    pallas_call x1, Pallas kernels, front(): pl.pallas_call(front_kernel, in_specs=[smem()] + [anywhere()] * 4, out_sp...  5.56 us
    pallas_call x1, Pallas kernels, self_mix(): pl.pallas_call(functools.partial(norm_kernel, tuple(digits)), in_specs=[a...  4.5 us
    pallas_call x2, Pallas kernels, to_cross(): pl.pallas_call(functools.partial(across_kernel, len(tokens), len(states))...  4.37 us
  transfers between devices with their start and end apart: 17, of which 3 were waited for; matrix products, arithmetic and copies ran while one was open for 1% of the time, Pallas kernels for 45%

commit v1 on v0

--- a/solution.py
+++ b/solution.py
@@ -189,6 +189,9 @@
 
     @pl.when(i == 0)
     def _():
+        if first:
+            for t in range(tiles):
+                query_move(t).start()
         if last:
             for move in state_moves(0, True):
                 move.start()
@@ -225,9 +228,11 @@
         for t in range(tiles):
             found[t] = lengths[t]
 
-            @pl.when(lengths[t] > 0)
-            def _():
-                query_move(t).start()
+            if not first:
+
+                @pl.when(lengths[t] > 0)
+                def _():
+                    query_move(t).start()
 
             if not first and not (last and t == 0):
 
@@ -704,12 +709,14 @@
         lambda c: [c, pick(c, (1, 1), (3, 1))],
         state,
         False,
-        waits=[across_v, gain_row],
+        waits=[across_v],
     )
 
     (swap_v,) = after([swap_v], state[0])
     summed = [own_sums, *partners] if len(digits) > 1 else []
-    across_k, up_k, *going = to_cross(late_k, up_k, state[0], up_v_beside, *partners, states=summed)
+    across_k, up_k, *going = to_cross(
+        late_k, up_k, state[0], up_v_beside, gain_row, *partners, states=summed
+    )
     swap_k = sent(across_k, swap)
     far_k = sent(up_k, further)
     far_v = sent(swap_v, onward)

time: 80.4 us -> 81 us (level)
  the two profiles are of different devices: /device:TPU:16 before, /device:TPU:18 now
where the time goes in v1:
time: 81 us
  Pallas kernels  45.2 us (56%)
  waiting for transfers between devices  19.2 us (24%)
  starting transfers between devices  15 us (19%)
  between operations  0.94 us (1%)
    pallas_call x4, Pallas kernels, attend(): pl.pallas_call(functools.partial(attend_kernel, setup), grid=(tiles,), in...  30.8 us
    ppermute x17, waiting for transfers between devices, sent(): return lax.ppermute(block, 'tm', pairs)  19.2 us
    ppermute x17, starting transfers between devices, sent(): return lax.ppermute(block, 'tm', pairs)  15 us
    pallas_call x1, Pallas kernels, front(): pl.pallas_call(front_kernel, in_specs=[smem()] + [anywhere()] * 4, out_sp...  5.55 us
    pallas_call x1, Pallas kernels, self_mix(): pl.pallas_call(functools.partial(norm_kernel, tuple(digits)), in_specs=[a...  4.5 us
    pallas_call x2, Pallas kernels, to_cross(): pl.pallas_call(functools.partial(across_kernel, len(tokens), len(states))...  4.37 us
  transfers between devices with their start and end apart: 17, of which 4 were waited for; matrix products, arithmetic and copies ran while one was open for 1% of the time, Pallas kernels for 38%

profile of v1, /device:TPU:18, one launch (start us, length us, event | category | flops | bytes accessed | tf_op | source)
XLA Modules:
  0.0 81.0 jit_solution(18336511872471461581)
XLA Ops:
  0.6 0.1 collective-permute-start.4
  0.7 1.6 %collective-permute-start.3 = (bf16[2240,128]{1,0:T(8,128)(2,1)}, bf16[2240,128]{1,0:T(8,128)(2,1)}, u32[]{:S(2)}, u32[]{:S(2)}) collective-permute-start(bf16[2240,128]{1,0:T(8,128)(2,1)} %bitcast.22), channel_id=1, source_target_pairs={{0,4},{1,5},{2,6},{3,7},{4,8},{5,9},{6,10},{7,11},{8,12},{9,13},{1... | collective-permute-start | bytes 1720328 | tf_op jit(solution)/shard_map/ppermute | solution.py:645
  2.3 5.6 %front.1 = (f32[18,32,128]{2,1,0:T(8,128)}, bf16[18,32,128]{2,1,0:T(8,128)(2,1)}, bf16[18,128,128]{2,1,0:T(8,128)(2,1)}, bf16[18,128,128]{2,1,0:T(8,128)(2,1)}) custom-call(s32[16]{0:T(128)} %tokens_ref.9, bf16[2240,384]{1,0:T(8,128)(2,1)} %bitcast.15, bf16[2240,384]{1,0:T(8,128)(2,1)} %bitcast.16, bf16[2240,128]{1,0:T(8,128)(2,1)} %bitcast.19, ...), custom_call_target="tpu_custom_call" | custom-call | flops 880803 | bytes 3440 | tf_op jit(solution)/shard_map/front/pallas_call | solution.py:499
  7.9 0.2 collective-permute-start
  8.1 1.5 %collective-permute-start.1 = (bf16[18,32,128]{2,1,0:T(8,128)(2,1)}, bf16[18,32,128]{2,1,0:T(8,128)(2,1)}, u32[]{:S(2)}, u32[]{:S(2)}) collective-permute-start(bf16[18,32,128]{2,1,0:T(8,128)(2,1)} %get-tuple-element.21.refs_3_), channel_id=1, source_target_pairs={{0,2},{1,3},{2,0},{3,1},{4,6},{5,7},{6,4},{7,5},{8,10},{9,11},{10,... | collective-permute-start | bytes 442376 | tf_op jit(solution)/shard_map/ppermute | solution.py:645
  9.6 0.2 collective-permute-start.2
  9.8 9.4 %attend.4 = (f32[3,18,4,256]{3,2,1,0:T(4,128)}, f32[3,18,64,256]{3,2,1,0:T(8,128)}) custom-call(s32[16]{0:T(128)} %start_ref.7, s32[16]{0:T(128)} %end_ref.7, s32[16]{0:T(128)} %tokens_ref.9, s32[3,16]{1,0:T(4,128)} %bitcast.30, bf16[2240,384]{1,0:T(8,128)(2,1)} %bitcast.25, bf16[18,128,128]{2,1,0:T(8,128)(2,1)} %get-tuple-element.22.refs_1_, ...), custom_call_target="tpu_custom_call" | custom-call | flops 4404019 | bytes 3440 | tf_op jit(solution)/shard_map/attend/pallas_call | solution.py:426
  19.3 0.0 copy-start
  19.3 0.0 collective-permute-done.refs_2_.refs_6_.refs_3_.refs_8_.refs_0_
  19.3 0.5 collective-permute-start.7
  19.8 0.0 collective-permute-done.1.refs_3_.refs_7_.refs_4_.refs_9_.refs_1_
  19.8 0.3 collective-permute-start.6
  20.1 0.0 collective-permute-done.2.refs_4_.refs_8_.refs_5_.refs_10_.refs_2_
  20.1 0.0 collective-permute-done.4.refs_1_.refs_4_
  20.1 0.0 collective-permute-done.3.up_hbm
  20.1 2.2 %to_cross.2 = (bf16[2240,128]{1,0:T(8,128)(2,1)}, bf16[2240,128]{1,0:T(8,128)(2,1)}, bf16[18,32,128]{2,1,0:T(8,128)(2,1)}) custom-call(bf16[2240,128]{1,0:T(8,128)(2,1)} %bitcast.23, bf16[2240,128]{1,0:T(8,128)(2,1)} %collective-permute-done.3.up_hbm, f32[3,18,4,256]{3,2,1,0:T(4,128)} %get-tuple-element.23.refs_0_.refs_1_.refs_6_, ...), custom_call_target="tpu_custom_call", output_to_operand_aliasing={{1}: (1, {})} | custom-call | bytes 1146 | tf_op jit(solution)/shard_map/to_cross/pallas_call | solution.py:140
  22.3 0.1 collective-permute-start.8
  22.3 1.6 %collective-permute-start.11 = (bf16[2240,128]{1,0:T(8,128)(2,1)}, bf16[2240,128]{1,0:T(8,128)(2,1)}, u32[]{:S(2)}, u32[]{:S(2)}) collective-permute-start(bf16[2240,128]{1,0:T(8,128)(2,1)} %get-tuple-element.26.refs_5_), channel_id=1, source_target_pairs={{0,2},{1,3},{2,0},{3,1},{4,6},{5,7},{6,4},{7,5},{8,10},{9,11},{10,... | collective-permute-start | bytes 1720328 | tf_op jit(solution)/shard_map/ppermute | solution.py:645
  23.9 1.5 %collective-permute-start.5 = (bf16[18,32,128]{2,1,0:T(8,128)(2,1)}, bf16[18,32,128]{2,1,0:T(8,128)(2,1)}, u32[]{:S(2)}, u32[]{:S(2)}) collective-permute-start(bf16[18,32,128]{2,1,0:T(8,128)(2,1)} %get-tuple-element.24), channel_id=1, source_target_pairs={{0,4},{1,5},{2,6},{3,7},{4,0},{5,1},{6,2},{7,3},{8,12},{9,13},{10,... | collective-permute-start | bytes 442376 | tf_op jit(solution)/shard_map/ppermute | solution.py:645
  25.4 0.0 copy-done
  25.4 0.6 reshape.13.refs_2_.gain_hbm
  26.0 0.0 collective-permute-done.7.refs_2_
  26.0 1.1 %attend.5 = (f32[3,18,4,256]{3,2,1,0:T(4,128)}, f32[3,18,64,256]{3,2,1,0:T(8,128)}) custom-call(s32[16]{0:T(128)} %start_ref.7, s32[16]{0:T(128)} %end_ref.7, s32[16]{0:T(128)} %tokens_ref.9, s32[3,16]{1,0:T(4,128)} %bitcast.31, bf16[2240,384]{1,0:T(8,128)(2,1)} %bitcast.26, ...), custom_call_target="tpu_custom_call", output_to_operand_aliasing={{0}: (10, {}), {1}: (11, {})} | custom-call | flops 8808038 | bytes 3440 | tf_op jit(solution)/shard_map/attend/pallas_call | solution.py:426
  27.2 8.2 %collective-permute-done.6.up_hbm = bf16[18,128,128]{2,1,0:T(8,128)(2,1)} collective-permute-done((bf16[18,128,128]{2,1,0:T(8,128)(2,1)}, bf16[18,128,128]{2,1,0:T(8,128)(2,1)}, u32[]{:S(2)}, u32[]{:S(2)}) %collective-permute-start.6) | collective-permute-done | bytes 589856 | tf_op jit(solution)/shard_map/ppermute | solution.py:645
  35.4 2.9 %collective-permute-done.5.refs_6_.refs_11_.refs_3_ = bf16[18,32,128]{2,1,0:T(8,128)(2,1)} collective-permute-done((bf16[18,32,128]{2,1,0:T(8,128)(2,1)}, bf16[18,32,128]{2,1,0:T(8,128)(2,1)}, u32[]{:S(2)}, u32[]{:S(2)}) %collective-permute-start.5) | collective-permute-done | bytes 147488 | tf_op jit(solution)/shard_map/ppermute | solution.py:645
  38.3 0.0 collective-permute-done.8.refs_1_.refs_4_
  38.4 2.2 %to_cross.3 = (bf16[18,128,128]{2,1,0:T(8,128)(2,1)}, bf16[18,128,128]{2,1,0:T(8,128)(2,1)}, bf16[18,32,128]{2,1,0:T(8,128)(2,1)}) custom-call(bf16[18,128,128]{2,1,0:T(8,128)(2,1)} %after.3.refs_1_.own_hbm, bf16[18,128,128]{2,1,0:T(8,128)(2,1)} %collective-permute-done.6.up_hbm, ...), custom_call_target="tpu_custom_call", output_to_operand_aliasing={{1}: (1, {})} | custom-call | bytes 1179 | tf_op jit(solution)/shard_map/to_cross/pallas_call | solution.py:140
  40.6 0.1 collective-permute-start.12
  40.6 1.6 %collective-permute-start.10 = (bf16[18,128,128]{2,1,0:T(8,128)(2,1)}, bf16[18,128,128]{2,1,0:T(8,128)(2,1)}, u32[]{:S(2)}, u32[]{:S(2)}) collective-permute-start(bf16[18,128,128]{2,1,0:T(8,128)(2,1)} %get-tuple-element.31.refs_5_), channel_id=1, source_target_pairs={{0,2},{1,3},{2,0},{3,1},{4,6},{5,7},{6,4},{7,5},{8,10},{9,11},{10,... | collective-permute-start | bytes 1769480 | tf_op jit(solution)/shard_map/ppermute | solution.py:645
  42.2 0.0 collective-permute-done.11.refs_0_
  42.2 1.3 %collective-permute-start.13 = (bf16[2240,128]{1,0:T(8,128)(2,1)}, bf16[2240,128]{1,0:T(8,128)(2,1)}, u32[]{:S(2)}, u32[]{:S(2)}) collective-permute-start(bf16[2240,128]{1,0:T(8,128)(2,1)} %after.4.refs_1_), channel_id=1, source_target_pairs={{1,4},{3,6},{5,8},{7,10},{9,12},{11,14},{17,20},{19,22},{21,24},{2... | collective-permute-start | bytes 1720328 | tf_op jit(solution)/shard_map/ppermute | solution.py:645
  43.5 2.5 %collective-permute-start.9 = (bf16[18,32,128]{2,1,0:T(8,128)(2,1)}, bf16[18,32,128]{2,1,0:T(8,128)(2,1)}, u32[]{:S(2)}, u32[]{:S(2)}) collective-permute-start(bf16[18,32,128]{2,1,0:T(8,128)(2,1)} %get-tuple-element.30), channel_id=1, source_target_pairs={{0,8},{1,9},{2,10},{3,11},{4,12},{5,13},{6,14},{7,15},{8,0},{9,1},... | collective-permute-start | bytes 442376 | tf_op jit(solution)/shard_map/ppermute | solution.py:645
  46.1 1.5 %collective-permute-start.15 = (bf16[18,128,128]{2,1,0:T(8,128)(2,1)}, bf16[18,128,128]{2,1,0:T(8,128)(2,1)}, u32[]{:S(2)}, u32[]{:S(2)}) collective-permute-start(bf16[18,128,128]{2,1,0:T(8,128)(2,1)} %get-tuple-element.32.refs_1_), channel_id=1, source_target_pairs={{1,2},{3,4},{5,6},{7,8},{9,10},{11,12},{13,14},{17,18},{19,20},{21... | collective-permute-start | bytes 1769480 | tf_op jit(solution)/shard_map/ppermute | solution.py:645
  47.5 0.0 collective-permute-done.12.refs_2_
  47.5 5.6 %attend.6 = (f32[3,18,4,256]{3,2,1,0:T(4,128)}, f32[3,18,64,256]{3,2,1,0:T(8,128)}) custom-call(s32[16]{0:T(128)} %start_ref.7, s32[16]{0:T(128)} %end_ref.7, s32[16]{0:T(128)} %tokens_ref.9, s32[3,16]{1,0:T(4,128)} %bitcast.32, bf16[2240,384]{1,0:T(8,128)(2,1)} %bitcast.27, ...), custom_call_target="tpu_custom_call", output_to_operand_aliasing={{0}: (10, {}), {1}: (11, {})} | custom-call | flops 8808038 | bytes 3440 | tf_op jit(solution)/shard_map/attend/pallas_call | solution.py:426
  53.1 0.0 collective-permute-done.9.refs_4_
  53.2 5.1 %collective-permute-done.13.refs_3_.refs_6_ = bf16[2240,128]{1,0:T(8,128)(2,1)} collective-permute-done((bf16[2240,128]{1,0:T(8,128)(2,1)}, bf16[2240,128]{1,0:T(8,128)(2,1)}, u32[]{:S(2)}, u32[]{:S(2)}) %collective-permute-start.13) | collective-permute-done | bytes 573472 | tf_op jit(solution)/shard_map/ppermute | solution.py:645
  58.3 0.0 collective-permute-done.10.refs_0_
  58.3 0.0 collective-permute-start.14
  58.3 0.5 collective-permute-start.16
  58.8 4.5 %self_mix.1.refs_7_ = bf16[2240,384]{1,0:T(8,128)(2,1)} custom-call(bf16[2240,384]{1,0:T(8,128)(2,1)} %bitcast.17, f32[1,2240]{1,0:T(1,128)} %reshape.13.refs_2_.gain_hbm, f32[18,32,128]{2,1,0:T(8,128)} %get-tuple-element.20.refs_5_.refs_7_.own_hbm, bf16[18,32,128]{2,1,0:T(8,128)(2,1)} %collective-permute-done.refs_2_.refs_6_.refs_3_.refs_8_.refs_0_, ...), custom_call_target="tpu_custom_call" | custom-call | flops 880803 | bytes 3440 | tf_op jit(solution)/shard_map/self_mix/pallas_call | solution.py:622
  63.3 2.9 %collective-permute-done.15.refs_3_ = bf16[18,128,128]{2,1,0:T(8,128)(2,1)} collective-permute-done((bf16[18,128,128]{2,1,0:T(8,128)(2,1)}, bf16[18,128,128]{2,1,0:T(8,128)(2,1)}, u32[]{:S(2)}, u32[]{:S(2)}) %collective-permute-start.15) | collective-permute-done | bytes 589856 | tf_op jit(solution)/shard_map/ppermute | solution.py:645
  66.2 0.0 collective-permute-done.16.refs_5_
  66.2 0.0 collective-permute-done.14.refs_2_
  66.2 14.7 %attend.7 = bf16[2240,384]{1,0:T(8,128)(2,1)} custom-call(s32[16]{0:T(128)} %start_ref.7, s32[16]{0:T(128)} %end_ref.7, s32[16]{0:T(128)} %tokens_ref.9, s32[3,16]{1,0:T(4,128)} %bitcast.33, bf16[2240,384]{1,0:T(8,128)(2,1)} %bitcast.28, bf16[18,128,128]{2,1,0:T(8,128)(2,1)} %get-tuple-element.35.refs_5_.refs_1_, ...), custom_call_target="tpu_custom_call" | custom-call | flops 13212057 | bytes 3440 | tf_op jit(solution)/shard_map/attend/pallas_call | solution.py:426
  (3 shorter events, 0.0 us)
Async XLA Ops:
  0.6 19.5 %collective-permute-start.4 = (bf16[2240,128]{1,0:T(8,128)(2,1)}, bf16[2240,128]{1,0:T(8,128)(2,1)}, u32[]{:S(2)}, u32[]{:S(2)}) collective-permute-start(bf16[2240,128]{1,0:T(8,128)(2,1)} %bitcast.21), channel_id=1, source_target_pairs={{0,1},{1,0},{2,3},{3,2},{4,5},{5,4},{6,7},{7,6},{8,9},{9,8},{10,11... | collective-permute-start | bytes 1720328 | tf_op jit(solution)/shard_map/ppermute | solution.py:645
  0.7 19.4 %collective-permute-start.3 = (bf16[2240,128]{1,0:T(8,128)(2,1)}, bf16[2240,128]{1,0:T(8,128)(2,1)}, u32[]{:S(2)}, u32[]{:S(2)}) collective-permute-start(bf16[2240,128]{1,0:T(8,128)(2,1)} %bitcast.22), channel_id=1, source_target_pairs={{0,4},{1,5},{2,6},{3,7},{4,8},{5,9},{6,10},{7,11},{8,12},{9,13},{1... | collective-permute-start | bytes 1720328 | tf_op jit(solution)/shard_map/ppermute | solution.py:645
  7.9 11.4 %collective-permute-start = (bf16[18,32,128]{2,1,0:T(8,128)(2,1)}, bf16[18,32,128]{2,1,0:T(8,128)(2,1)}, u32[]{:S(2)}, u32[]{:S(2)}) collective-permute-start(bf16[18,32,128]{2,1,0:T(8,128)(2,1)} %get-tuple-element.21.refs_3_), channel_id=1, source_target_pairs={{0,1},{1,0},{2,3},{3,2},{4,5},{5,4},{6,7},{7,6},{8,9},{9,8},{10,11... | collective-permute-start | bytes 442376 | tf_op jit(solution)/shard_map/ppermute | solution.py:645
  8.1 11.7 %collective-permute-start.1 = (bf16[18,32,128]{2,1,0:T(8,128)(2,1)}, bf16[18,32,128]{2,1,0:T(8,128)(2,1)}, u32[]{:S(2)}, u32[]{:S(2)}) collective-permute-start(bf16[18,32,128]{2,1,0:T(8,128)(2,1)} %get-tuple-element.21.refs_3_), channel_id=1, source_target_pairs={{0,2},{1,3},{2,0},{3,1},{4,6},{5,7},{6,4},{7,5},{8,10},{9,11},{10,... | collective-permute-start | bytes 442376 | tf_op jit(solution)/shard_map/ppermute | solution.py:645
  9.6 10.4 %collective-permute-start.2 = (bf16[18,32,128]{2,1,0:T(8,128)(2,1)}, bf16[18,32,128]{2,1,0:T(8,128)(2,1)}, u32[]{:S(2)}, u32[]{:S(2)}) collective-permute-start(bf16[18,32,128]{2,1,0:T(8,128)(2,1)} %get-tuple-element.21.refs_3_), channel_id=1, source_target_pairs={{0,3},{1,2},{2,1},{3,0},{4,7},{5,6},{6,5},{7,4},{8,11},{9,10},{10,... | collective-permute-start | bytes 442376 | tf_op jit(solution)/shard_map/ppermute | solution.py:645
  19.3 6.2 %copy-start = (f32[2240]{0:T(1024)S(1)}, f32[2240]{0:T(1024)}, u32[]{:S(2)}) copy-start(f32[2240]{0:T(1024)} %param.25) | copy-start | bytes 26884
  19.3 6.8 %collective-permute-start.7 = (bf16[18,128,128]{2,1,0:T(8,128)(2,1)}, bf16[18,128,128]{2,1,0:T(8,128)(2,1)}, u32[]{:S(2)}, u32[]{:S(2)}) collective-permute-start(bf16[18,128,128]{2,1,0:T(8,128)(2,1)} %after.3.refs_1_.own_hbm), channel_id=1, source_target_pairs={{0,1},{1,0},{2,3},{3,2},{4,5},{5,4},{6,7},{7,6},{8,9},{9,8},{10,11... | collective-permute-start | bytes 1769480 | tf_op jit(solution)/shard_map/ppermute | solution.py:645
  19.8 15.6 %collective-permute-start.6 = (bf16[18,128,128]{2,1,0:T(8,128)(2,1)}, bf16[18,128,128]{2,1,0:T(8,128)(2,1)}, u32[]{:S(2)}, u32[]{:S(2)}) collective-permute-start(bf16[18,128,128]{2,1,0:T(8,128)(2,1)} %after.3.refs_1_.own_hbm), channel_id=1, source_target_pairs={{0,4},{1,5},{2,6},{3,7},{4,8},{5,9},{6,10},{7,11},{8,12},{9,13},{1... | collective-permute-start | bytes 1769480 | tf_op jit(solution)/shard_map/ppermute | solution.py:645
  22.3 16.1 %collective-permute-start.8 = (bf16[2240,128]{1,0:T(8,128)(2,1)}, bf16[2240,128]{1,0:T(8,128)(2,1)}, u32[]{:S(2)}, u32[]{:S(2)}) collective-permute-start(bf16[2240,128]{1,0:T(8,128)(2,1)} %get-tuple-element.29.refs_3_), channel_id=1, source_target_pairs={{0,1},{1,0},{2,3},{3,2},{4,5},{5,4},{6,7},{7,6},{8,9},{9,8},{10,11... | collective-permute-start | bytes 1720328 | tf_op jit(solution)/shard_map/ppermute | solution.py:645
  22.3 19.9 %collective-permute-start.11 = (bf16[2240,128]{1,0:T(8,128)(2,1)}, bf16[2240,128]{1,0:T(8,128)(2,1)}, u32[]{:S(2)}, u32[]{:S(2)}) collective-permute-start(bf16[2240,128]{1,0:T(8,128)(2,1)} %get-tuple-element.26.refs_5_), channel_id=1, source_target_pairs={{0,2},{1,3},{2,0},{3,1},{4,6},{5,7},{6,4},{7,5},{8,10},{9,11},{10,... | collective-permute-start | bytes 1720328 | tf_op jit(solution)/shard_map/ppermute | solution.py:645
  23.9 14.4 %collective-permute-start.5 = (bf16[18,32,128]{2,1,0:T(8,128)(2,1)}, bf16[18,32,128]{2,1,0:T(8,128)(2,1)}, u32[]{:S(2)}, u32[]{:S(2)}) collective-permute-start(bf16[18,32,128]{2,1,0:T(8,128)(2,1)} %get-tuple-element.24), channel_id=1, source_target_pairs={{0,4},{1,5},{2,6},{3,7},{4,0},{5,1},{6,2},{7,3},{8,12},{9,13},{10,... | collective-permute-start | bytes 442376 | tf_op jit(solution)/shard_map/ppermute | solution.py:645
  40.6 7.0 %collective-permute-start.12 = (bf16[18,128,128]{2,1,0:T(8,128)(2,1)}, bf16[18,128,128]{2,1,0:T(8,128)(2,1)}, u32[]{:S(2)}, u32[]{:S(2)}) collective-permute-start(bf16[18,128,128]{2,1,0:T(8,128)(2,1)} %get-tuple-element.32.refs_1_), channel_id=1, source_target_pairs={{0,1},{1,0},{2,3},{3,2},{4,5},{5,4},{6,7},{7,6},{8,9},{9,8},{10,11... | collective-permute-start | bytes 1769480 | tf_op jit(solution)/shard_map/ppermute | solution.py:645
  40.6 17.7 %collective-permute-start.10 = (bf16[18,128,128]{2,1,0:T(8,128)(2,1)}, bf16[18,128,128]{2,1,0:T(8,128)(2,1)}, u32[]{:S(2)}, u32[]{:S(2)}) collective-permute-start(bf16[18,128,128]{2,1,0:T(8,128)(2,1)} %get-tuple-element.31.refs_5_), channel_id=1, source_target_pairs={{0,2},{1,3},{2,0},{3,1},{4,6},{5,7},{6,4},{7,5},{8,10},{9,11},{10,... | collective-permute-start | bytes 1769480 | tf_op jit(solution)/shard_map/ppermute | solution.py:645
  42.2 16.1 %collective-permute-start.13 = (bf16[2240,128]{1,0:T(8,128)(2,1)}, bf16[2240,128]{1,0:T(8,128)(2,1)}, u32[]{:S(2)}, u32[]{:S(2)}) collective-permute-start(bf16[2240,128]{1,0:T(8,128)(2,1)} %after.4.refs_1_), channel_id=1, source_target_pairs={{1,4},{3,6},{5,8},{7,10},{9,12},{11,14},{17,20},{19,22},{21,24},{2... | collective-permute-start | bytes 1720328 | tf_op jit(solution)/shard_map/ppermute | solution.py:645
  43.5 9.6 %collective-permute-start.9 = (bf16[18,32,128]{2,1,0:T(8,128)(2,1)}, bf16[18,32,128]{2,1,0:T(8,128)(2,1)}, u32[]{:S(2)}, u32[]{:S(2)}) collective-permute-start(bf16[18,32,128]{2,1,0:T(8,128)(2,1)} %get-tuple-element.30), channel_id=1, source_target_pairs={{0,8},{1,9},{2,10},{3,11},{4,12},{5,13},{6,14},{7,15},{8,0},{9,1},... | collective-permute-start | bytes 442376 | tf_op jit(solution)/shard_map/ppermute | solution.py:645
  46.1 20.1 %collective-permute-start.15 = (bf16[18,128,128]{2,1,0:T(8,128)(2,1)}, bf16[18,128,128]{2,1,0:T(8,128)(2,1)}, u32[]{:S(2)}, u32[]{:S(2)}) collective-permute-start(bf16[18,128,128]{2,1,0:T(8,128)(2,1)} %get-tuple-element.32.refs_1_), channel_id=1, source_target_pairs={{1,2},{3,4},{5,6},{7,8},{9,10},{11,12},{13,14},{17,18},{19,20},{21... | collective-permute-start | bytes 1769480 | tf_op jit(solution)/shard_map/ppermute | solution.py:645
  58.3 7.9 %collective-permute-start.14 = (bf16[18,128,128]{2,1,0:T(8,128)(2,1)}, bf16[18,128,128]{2,1,0:T(8,128)(2,1)}, u32[]{:S(2)}, u32[]{:S(2)}) collective-permute-start(bf16[18,128,128]{2,1,0:T(8,128)(2,1)} %get-tuple-element.35.refs_5_.refs_1_), channel_id=1, source_target_pairs={{0,1},{1,0},{2,3},{3,2},{4,5},{5,4},{6,7},{7,6},{8,9},{9,8},{10,11... | collective-permute-start | bytes 1769480 | tf_op jit(solution)/shard_map/ppermute | solution.py:645
  58.3 7.9 %collective-permute-start.16 = (bf16[2240,128]{1,0:T(8,128)(2,1)}, bf16[2240,128]{1,0:T(8,128)(2,1)}, u32[]{:S(2)}, u32[]{:S(2)}) collective-permute-start(bf16[2240,128]{1,0:T(8,128)(2,1)} %get-tuple-element.36.refs_4_), channel_id=1, source_target_pairs={{0,1},{1,0},{2,3},{3,2},{4,5},{5,4},{6,7},{7,6},{8,9},{9,8},{10,11... | collective-permute-start | bytes 1720328 | tf_op jit(solution)/shard_map/ppermute | solution.py:645

commit v2 on v1

--- a/solution.py
+++ b/solution.py
@@ -730,7 +730,7 @@
         waits=[across_k],
     )
 
-    swap_k, swap_v = after([swap_k, swap_v], state[0], far_v, *final)
+    swap_k, swap_v = after([swap_k, swap_v], state[0], *final)
     swap_k_beside = sent(swap_k, beside)
     swap_v_beside = sent(swap_v, beside)
     self_mixed = self_mix(jnp.transpose(queries), own_sums, gain_row, partners + final, digits, swap_k)

time: 81 us -> 81.9 us (1.011)
  the two profiles are of different devices: /device:TPU:18 before, /device:TPU:26 now
where the time goes in v2:
time: 81.9 us; the launch traced here: 83 us
  Pallas kernels  55.9 us (68%)
  starting transfers between devices  13.1 us (16%)
  waiting for transfers between devices  12.5 us (15%)
  between operations  0.97 us (1%)
    pallas_call x4, Pallas kernels, attend(): pl.pallas_call(functools.partial(attend_kernel, setup), grid=(tiles,), in...  41.4 us
    ppermute x17, starting transfers between devices, sent(): return lax.ppermute(block, 'tm', pairs)  13.1 us
    ppermute x17, waiting for transfers between devices, sent(): return lax.ppermute(block, 'tm', pairs)  12.5 us
    pallas_call x1, Pallas kernels, front(): pl.pallas_call(front_kernel, in_specs=[smem()] + [anywhere()] * 4, out_sp...  5.56 us
    pallas_call x1, Pallas kernels, self_mix(): pl.pallas_call(functools.partial(norm_kernel, tuple(digits)), in_specs=[a...  4.5 us
    pallas_call x2, Pallas kernels, to_cross(): pl.pallas_call(functools.partial(across_kernel, len(tokens), len(states))...  4.37 us
  transfers between devices with their start and end apart: 17, of which 4 were waited for; matrix products, arithmetic and copies ran while one was open for 1% of the time, Pallas kernels for 46%

profile of v2, /device:TPU:26, one launch (start us, length us, event | category | flops | bytes accessed | tf_op | source)
XLA Modules:
  0.0 83.0 jit_solution(17424538185382883805)
XLA Ops:
  0.6 0.1 collective-permute-start.4
  0.7 0.3 collective-permute-start.3
  1.0 5.6 %front.1 = (f32[18,32,128]{2,1,0:T(8,128)}, bf16[18,32,128]{2,1,0:T(8,128)(2,1)}, bf16[18,128,128]{2,1,0:T(8,128)(2,1)}, bf16[18,128,128]{2,1,0:T(8,128)(2,1)}) custom-call(s32[16]{0:T(128)} %tokens_ref.9, bf16[2240,384]{1,0:T(8,128)(2,1)} %bitcast.15, bf16[2240,384]{1,0:T(8,128)(2,1)} %bitcast.16, bf16[2240,128]{1,0:T(8,128)(2,1)} %bitcast.19, ...), custom_call_target="tpu_custom_call" | custom-call | flops 880803 | bytes 3440 | tf_op jit(solution)/shard_map/front/pallas_call | solution.py:499
  6.6 0.3 collective-permute-start
  6.8 1.5 %collective-permute-start.1 = (bf16[18,32,128]{2,1,0:T(8,128)(2,1)}, bf16[18,32,128]{2,1,0:T(8,128)(2,1)}, u32[]{:S(2)}, u32[]{:S(2)}) collective-permute-start(bf16[18,32,128]{2,1,0:T(8,128)(2,1)} %get-tuple-element.21.refs_3_), channel_id=1, source_target_pairs={{0,2},{1,3},{2,0},{3,1},{4,6},{5,7},{6,4},{7,5},{8,10},{9,11},{10,... | collective-permute-start | bytes 442376 | tf_op jit(solution)/shard_map/ppermute | solution.py:645
  8.4 0.1 collective-permute-start.2
  8.5 9.4 %attend.4 = (f32[3,18,4,256]{3,2,1,0:T(4,128)}, f32[3,18,64,256]{3,2,1,0:T(8,128)}) custom-call(s32[16]{0:T(128)} %start_ref.7, s32[16]{0:T(128)} %end_ref.7, s32[16]{0:T(128)} %tokens_ref.9, s32[3,16]{1,0:T(4,128)} %bitcast.30, bf16[2240,384]{1,0:T(8,128)(2,1)} %bitcast.25, bf16[18,128,128]{2,1,0:T(8,128)(2,1)} %get-tuple-element.22.refs_1_, ...), custom_call_target="tpu_custom_call" | custom-call | flops 4404019 | bytes 3440 | tf_op jit(solution)/shard_map/attend/pallas_call | solution.py:426
  17.9 0.0 copy-start
  17.9 0.0 collective-permute-done.refs_2_.refs_6_.refs_3_.refs_8_.refs_0_
  17.9 0.6 collective-permute-start.7
  18.5 0.0 collective-permute-done.1.refs_3_.refs_7_.refs_4_.refs_9_.refs_1_
  18.5 1.5 %collective-permute-start.6 = (bf16[18,128,128]{2,1,0:T(8,128)(2,1)}, bf16[18,128,128]{2,1,0:T(8,128)(2,1)}, u32[]{:S(2)}, u32[]{:S(2)}) collective-permute-start(bf16[18,128,128]{2,1,0:T(8,128)(2,1)} %after.3.refs_1_.own_hbm), channel_id=1, source_target_pairs={{0,4},{1,5},{2,6},{3,7},{4,8},{5,9},{6,10},{7,11},{8,12},{9,13},{1... | collective-permute-start | bytes 1769480 | tf_op jit(solution)/shard_map/ppermute | solution.py:645
  20.0 0.0 collective-permute-done.2.refs_4_.refs_8_.refs_5_.refs_10_.refs_2_
  20.0 0.0 collective-permute-done.4.refs_1_.refs_4_
  20.0 0.0 collective-permute-done.3.up_hbm
  20.0 2.2 %to_cross.2 = (bf16[2240,128]{1,0:T(8,128)(2,1)}, bf16[2240,128]{1,0:T(8,128)(2,1)}, bf16[18,32,128]{2,1,0:T(8,128)(2,1)}) custom-call(bf16[2240,128]{1,0:T(8,128)(2,1)} %bitcast.23, bf16[2240,128]{1,0:T(8,128)(2,1)} %collective-permute-done.3.up_hbm, f32[3,18,4,256]{3,2,1,0:T(4,128)} %get-tuple-element.23.refs_0_.refs_1_.refs_6_, ...), custom_call_target="tpu_custom_call", output_to_operand_aliasing={{1}: (1, {})} | custom-call | bytes 1146 | tf_op jit(solution)/shard_map/to_cross/pallas_call | solution.py:140
  22.2 0.1 collective-permute-start.8
  22.3 1.6 %collective-permute-start.11 = (bf16[2240,128]{1,0:T(8,128)(2,1)}, bf16[2240,128]{1,0:T(8,128)(2,1)}, u32[]{:S(2)}, u32[]{:S(2)}) collective-permute-start(bf16[2240,128]{1,0:T(8,128)(2,1)} %get-tuple-element.26.refs_5_), channel_id=1, source_target_pairs={{0,2},{1,3},{2,0},{3,1},{4,6},{5,7},{6,4},{7,5},{8,10},{9,11},{10,... | collective-permute-start | bytes 1720328 | tf_op jit(solution)/shard_map/ppermute | solution.py:645
  23.9 0.5 collective-permute-start.5
  24.4 0.0 copy-done
  24.4 0.6 reshape.13.refs_2_.gain_hbm
  25.0 0.0 collective-permute-done.7.refs_2_
  25.0 5.8 %attend.5 = (f32[3,18,4,256]{3,2,1,0:T(4,128)}, f32[3,18,64,256]{3,2,1,0:T(8,128)}) custom-call(s32[16]{0:T(128)} %start_ref.7, s32[16]{0:T(128)} %end_ref.7, s32[16]{0:T(128)} %tokens_ref.9, s32[3,16]{1,0:T(4,128)} %bitcast.31, bf16[2240,384]{1,0:T(8,128)(2,1)} %bitcast.26, ...), custom_call_target="tpu_custom_call", output_to_operand_aliasing={{0}: (10, {}), {1}: (11, {})} | custom-call | flops 8808038 | bytes 3440 | tf_op jit(solution)/shard_map/attend/pallas_call | solution.py:426
  30.8 4.2 %collective-permute-done.6.up_hbm = bf16[18,128,128]{2,1,0:T(8,128)(2,1)} collective-permute-done((bf16[18,128,128]{2,1,0:T(8,128)(2,1)}, bf16[18,128,128]{2,1,0:T(8,128)(2,1)}, u32[]{:S(2)}, u32[]{:S(2)}) %collective-permute-start.6) | collective-permute-done | bytes 589856 | tf_op jit(solution)/shard_map/ppermute | solution.py:645
  35.0 2.3 %collective-permute-done.5.refs_6_.refs_11_.refs_3_ = bf16[18,32,128]{2,1,0:T(8,128)(2,1)} collective-permute-done((bf16[18,32,128]{2,1,0:T(8,128)(2,1)}, bf16[18,32,128]{2,1,0:T(8,128)(2,1)}, u32[]{:S(2)}, u32[]{:S(2)}) %collective-permute-start.5) | collective-permute-done | bytes 147488 | tf_op jit(solution)/shard_map/ppermute | solution.py:645
  37.3 0.0 collective-permute-done.8.refs_1_.refs_4_
  37.3 2.2 %to_cross.3 = (bf16[18,128,128]{2,1,0:T(8,128)(2,1)}, bf16[18,128,128]{2,1,0:T(8,128)(2,1)}, bf16[18,32,128]{2,1,0:T(8,128)(2,1)}) custom-call(bf16[18,128,128]{2,1,0:T(8,128)(2,1)} %after.3.refs_1_.own_hbm, bf16[18,128,128]{2,1,0:T(8,128)(2,1)} %collective-permute-done.6.up_hbm, ...), custom_call_target="tpu_custom_call", output_to_operand_aliasing={{1}: (1, {})} | custom-call | bytes 1179 | tf_op jit(solution)/shard_map/to_cross/pallas_call | solution.py:140
  39.5 0.1 collective-permute-start.12
  39.6 1.6 %collective-permute-start.10 = (bf16[18,128,128]{2,1,0:T(8,128)(2,1)}, bf16[18,128,128]{2,1,0:T(8,128)(2,1)}, u32[]{:S(2)}, u32[]{:S(2)}) collective-permute-start(bf16[18,128,128]{2,1,0:T(8,128)(2,1)} %get-tuple-element.31.refs_5_), channel_id=1, source_target_pairs={{0,2},{1,3},{2,0},{3,1},{4,6},{5,7},{6,4},{7,5},{8,10},{9,11},{10,... | collective-permute-start | bytes 1769480 | tf_op jit(solution)/shard_map/ppermute | solution.py:645
  41.2 0.0 collective-permute-done.11.refs_0_
  41.2 1.3 %collective-permute-start.16 = (bf16[2240,128]{1,0:T(8,128)(2,1)}, bf16[2240,128]{1,0:T(8,128)(2,1)}, u32[]{:S(2)}, u32[]{:S(2)}) collective-permute-start(bf16[2240,128]{1,0:T(8,128)(2,1)} %after.4.refs_1_), channel_id=1, source_target_pairs={{1,4},{3,6},{5,8},{7,10},{9,12},{11,14},{17,20},{19,22},{21,24},{2... | collective-permute-start | bytes 1720328 | tf_op jit(solution)/shard_map/ppermute | solution.py:645
  42.4 1.7 %collective-permute-start.9 = (bf16[18,32,128]{2,1,0:T(8,128)(2,1)}, bf16[18,32,128]{2,1,0:T(8,128)(2,1)}, u32[]{:S(2)}, u32[]{:S(2)}) collective-permute-start(bf16[18,32,128]{2,1,0:T(8,128)(2,1)} %get-tuple-element.30), channel_id=1, source_target_pairs={{0,8},{1,9},{2,10},{3,11},{4,12},{5,13},{6,14},{7,15},{8,0},{9,1},... | collective-permute-start | bytes 442376 | tf_op jit(solution)/shard_map/ppermute | solution.py:645
  44.1 1.5 %collective-permute-start.14 = (bf16[18,128,128]{2,1,0:T(8,128)(2,1)}, bf16[18,128,128]{2,1,0:T(8,128)(2,1)}, u32[]{:S(2)}, u32[]{:S(2)}) collective-permute-start(bf16[18,128,128]{2,1,0:T(8,128)(2,1)} %get-tuple-element.32.refs_1_), channel_id=1, source_target_pairs={{1,2},{3,4},{5,6},{7,8},{9,10},{11,12},{13,14},{17,18},{19,20},{21... | collective-permute-start | bytes 1769480 | tf_op jit(solution)/shard_map/ppermute | solution.py:645
  45.6 0.0 collective-permute-done.12.refs_2_
  45.6 8.2 %attend.6 = (f32[3,18,4,256]{3,2,1,0:T(4,128)}, f32[3,18,64,256]{3,2,1,0:T(8,128)}) custom-call(s32[16]{0:T(128)} %start_ref.7, s32[16]{0:T(128)} %end_ref.7, s32[16]{0:T(128)} %tokens_ref.9, s32[3,16]{1,0:T(4,128)} %bitcast.32, bf16[2240,384]{1,0:T(8,128)(2,1)} %bitcast.27, ...), custom_call_target="tpu_custom_call", output_to_operand_aliasing={{0}: (10, {}), {1}: (11, {})} | custom-call | flops 8808038 | bytes 3440 | tf_op jit(solution)/shard_map/attend/pallas_call | solution.py:426
  53.9 0.0 collective-permute-done.9.refs_3_.refs_4_
  53.9 0.2 collective-permute-done.16.refs_6_
  54.1 5.7 %collective-permute-done.10.refs_0_ = bf16[18,128,128]{2,1,0:T(8,128)(2,1)} collective-permute-done((bf16[18,128,128]{2,1,0:T(8,128)(2,1)}, bf16[18,128,128]{2,1,0:T(8,128)(2,1)}, u32[]{:S(2)}, u32[]{:S(2)}) %collective-permute-start.10) | collective-permute-done | bytes 589856 | tf_op jit(solution)/shard_map/ppermute | solution.py:645
  59.8 0.2 collective-permute-start.13
  60.0 0.3 collective-permute-start.15
  60.3 4.5 %self_mix.1.refs_7_ = bf16[2240,384]{1,0:T(8,128)(2,1)} custom-call(bf16[2240,384]{1,0:T(8,128)(2,1)} %bitcast.17, f32[1,2240]{1,0:T(1,128)} %reshape.13.refs_2_.gain_hbm, f32[18,32,128]{2,1,0:T(8,128)} %get-tuple-element.20.refs_5_.refs_7_.own_hbm, bf16[18,32,128]{2,1,0:T(8,128)(2,1)} %collective-permute-done.refs_2_.refs_6_.refs_3_.refs_8_.refs_0_, ...), custom_call_target="tpu_custom_call" | custom-call | flops 880803 | bytes 3440 | tf_op jit(solution)/shard_map/self_mix/pallas_call | solution.py:622
  64.8 0.0 collective-permute-done.14.refs_3_
  64.8 0.0 collective-permute-done.15.refs_5_
  64.8 0.0 collective-permute-done.13.refs_2_
  64.8 18.0 %attend.7 = bf16[2240,384]{1,0:T(8,128)(2,1)} custom-call(s32[16]{0:T(128)} %start_ref.7, s32[16]{0:T(128)} %end_ref.7, s32[16]{0:T(128)} %tokens_ref.9, s32[3,16]{1,0:T(4,128)} %bitcast.33, bf16[2240,384]{1,0:T(8,128)(2,1)} %bitcast.28, bf16[18,128,128]{2,1,0:T(8,128)(2,1)} %get-tuple-element.35.refs_5_.refs_1_, ...), custom_call_target="tpu_custom_call" | custom-call | flops 13212057 | bytes 3440 | tf_op jit(solution)/shard_map/attend/pallas_call | solution.py:426
  (3 shorter events, 0.0 us)
Async XLA Ops:
  0.6 19.4 %collective-permute-start.4 = (bf16[2240,128]{1,0:T(8,128)(2,1)}, bf16[2240,128]{1,0:T(8,128)(2,1)}, u32[]{:S(2)}, u32[]{:S(2)}) collective-permute-start(bf16[2240,128]{1,0:T(8,128)(2,1)} %bitcast.21), channel_id=1, source_target_pairs={{0,1},{1,0},{2,3},{3,2},{4,5},{5,4},{6,7},{7,6},{8,9},{9,8},{10,11... | collective-permute-start | bytes 1720328 | tf_op jit(solution)/shard_map/ppermute | solution.py:645
  0.7 19.3 %collective-permute-start.3 = (bf16[2240,128]{1,0:T(8,128)(2,1)}, bf16[2240,128]{1,0:T(8,128)(2,1)}, u32[]{:S(2)}, u32[]{:S(2)}) collective-permute-start(bf16[2240,128]{1,0:T(8,128)(2,1)} %bitcast.22), channel_id=1, source_target_pairs={{0,4},{1,5},{2,6},{3,7},{4,8},{5,9},{6,10},{7,11},{8,12},{9,13},{1... | collective-permute-start | bytes 1720328 | tf_op jit(solution)/shard_map/ppermute | solution.py:645
  6.6 11.4 %collective-permute-start = (bf16[18,32,128]{2,1,0:T(8,128)(2,1)}, bf16[18,32,128]{2,1,0:T(8,128)(2,1)}, u32[]{:S(2)}, u32[]{:S(2)}) collective-permute-start(bf16[18,32,128]{2,1,0:T(8,128)(2,1)} %get-tuple-element.21.refs_3_), channel_id=1, source_target_pairs={{0,1},{1,0},{2,3},{3,2},{4,5},{5,4},{6,7},{7,6},{8,9},{9,8},{10,11... | collective-permute-start | bytes 442376 | tf_op jit(solution)/shard_map/ppermute | solution.py:645
  6.8 11.7 %collective-permute-start.1 = (bf16[18,32,128]{2,1,0:T(8,128)(2,1)}, bf16[18,32,128]{2,1,0:T(8,128)(2,1)}, u32[]{:S(2)}, u32[]{:S(2)}) collective-permute-start(bf16[18,32,128]{2,1,0:T(8,128)(2,1)} %get-tuple-element.21.refs_3_), channel_id=1, source_target_pairs={{0,2},{1,3},{2,0},{3,1},{4,6},{5,7},{6,4},{7,5},{8,10},{9,11},{10,... | collective-permute-start | bytes 442376 | tf_op jit(solution)/shard_map/ppermute | solution.py:645
  8.4 11.7 %collective-permute-start.2 = (bf16[18,32,128]{2,1,0:T(8,128)(2,1)}, bf16[18,32,128]{2,1,0:T(8,128)(2,1)}, u32[]{:S(2)}, u32[]{:S(2)}) collective-permute-start(bf16[18,32,128]{2,1,0:T(8,128)(2,1)} %get-tuple-element.21.refs_3_), channel_id=1, source_target_pairs={{0,3},{1,2},{2,1},{3,0},{4,7},{5,6},{6,5},{7,4},{8,11},{9,10},{10,... | collective-permute-start | bytes 442376 | tf_op jit(solution)/shard_map/ppermute | solution.py:645
  17.9 6.5 %copy-start = (f32[2240]{0:T(1024)S(1)}, f32[2240]{0:T(1024)}, u32[]{:S(2)}) copy-start(f32[2240]{0:T(1024)} %param.25) | copy-start | bytes 26884
  17.9 7.1 %collective-permute-start.7 = (bf16[18,128,128]{2,1,0:T(8,128)(2,1)}, bf16[18,128,128]{2,1,0:T(8,128)(2,1)}, u32[]{:S(2)}, u32[]{:S(2)}) collective-permute-start(bf16[18,128,128]{2,1,0:T(8,128)(2,1)} %after.3.refs_1_.own_hbm), channel_id=1, source_target_pairs={{0,1},{1,0},{2,3},{3,2},{4,5},{5,4},{6,7},{7,6},{8,9},{9,8},{10,11... | collective-permute-start | bytes 1769480 | tf_op jit(solution)/shard_map/ppermute | solution.py:645
  18.5 16.5 %collective-permute-start.6 = (bf16[18,128,128]{2,1,0:T(8,128)(2,1)}, bf16[18,128,128]{2,1,0:T(8,128)(2,1)}, u32[]{:S(2)}, u32[]{:S(2)}) collective-permute-start(bf16[18,128,128]{2,1,0:T(8,128)(2,1)} %after.3.refs_1_.own_hbm), channel_id=1, source_target_pairs={{0,4},{1,5},{2,6},{3,7},{4,8},{5,9},{6,10},{7,11},{8,12},{9,13},{1... | collective-permute-start | bytes 1769480 | tf_op jit(solution)/shard_map/ppermute | solution.py:645
  22.2 15.1 %collective-permute-start.8 = (bf16[2240,128]{1,0:T(8,128)(2,1)}, bf16[2240,128]{1,0:T(8,128)(2,1)}, u32[]{:S(2)}, u32[]{:S(2)}) collective-permute-start(bf16[2240,128]{1,0:T(8,128)(2,1)} %get-tuple-element.29.refs_3_), channel_id=1, source_target_pairs={{0,1},{1,0},{2,3},{3,2},{4,5},{5,4},{6,7},{7,6},{8,9},{9,8},{10,11... | collective-permute-start | bytes 1720328 | tf_op jit(solution)/shard_map/ppermute | solution.py:645
  22.3 18.9 %collective-permute-start.11 = (bf16[2240,128]{1,0:T(8,128)(2,1)}, bf16[2240,128]{1,0:T(8,128)(2,1)}, u32[]{:S(2)}, u32[]{:S(2)}) collective-permute-start(bf16[2240,128]{1,0:T(8,128)(2,1)} %get-tuple-element.26.refs_5_), channel_id=1, source_target_pairs={{0,2},{1,3},{2,0},{3,1},{4,6},{5,7},{6,4},{7,5},{8,10},{9,11},{10,... | collective-permute-start | bytes 1720328 | tf_op jit(solution)/shard_map/ppermute | solution.py:645
  23.9 13.4 %collective-permute-start.5 = (bf16[18,32,128]{2,1,0:T(8,128)(2,1)}, bf16[18,32,128]{2,1,0:T(8,128)(2,1)}, u32[]{:S(2)}, u32[]{:S(2)}) collective-permute-start(bf16[18,32,128]{2,1,0:T(8,128)(2,1)} %get-tuple-element.24), channel_id=1, source_target_pairs={{0,4},{1,5},{2,6},{3,7},{4,0},{5,1},{6,2},{7,3},{8,12},{9,13},{10,... | collective-permute-start | bytes 442376 | tf_op jit(solution)/shard_map/ppermute | solution.py:645
  39.5 6.1 %collective-permute-start.12 = (bf16[18,128,128]{2,1,0:T(8,128)(2,1)}, bf16[18,128,128]{2,1,0:T(8,128)(2,1)}, u32[]{:S(2)}, u32[]{:S(2)}) collective-permute-start(bf16[18,128,128]{2,1,0:T(8,128)(2,1)} %get-tuple-element.32.refs_1_), channel_id=1, source_target_pairs={{0,1},{1,0},{2,3},{3,2},{4,5},{5,4},{6,7},{7,6},{8,9},{9,8},{10,11... | collective-permute-start | bytes 1769480 | tf_op jit(solution)/shard_map/ppermute | solution.py:645
  39.6 20.2 %collective-permute-start.10 = (bf16[18,128,128]{2,1,0:T(8,128)(2,1)}, bf16[18,128,128]{2,1,0:T(8,128)(2,1)}, u32[]{:S(2)}, u32[]{:S(2)}) collective-permute-start(bf16[18,128,128]{2,1,0:T(8,128)(2,1)} %get-tuple-element.31.refs_5_), channel_id=1, source_target_pairs={{0,2},{1,3},{2,0},{3,1},{4,6},{5,7},{6,4},{7,5},{8,10},{9,11},{10,... | collective-permute-start | bytes 1769480 | tf_op jit(solution)/shard_map/ppermute | solution.py:645
  41.2 12.9 %collective-permute-start.16 = (bf16[2240,128]{1,0:T(8,128)(2,1)}, bf16[2240,128]{1,0:T(8,128)(2,1)}, u32[]{:S(2)}, u32[]{:S(2)}) collective-permute-start(bf16[2240,128]{1,0:T(8,128)(2,1)} %after.4.refs_1_), channel_id=1, source_target_pairs={{1,4},{3,6},{5,8},{7,10},{9,12},{11,14},{17,20},{19,22},{21,24},{2... | collective-permute-start | bytes 1720328 | tf_op jit(solution)/shard_map/ppermute | solution.py:645
  42.4 11.4 %collective-permute-start.9 = (bf16[18,32,128]{2,1,0:T(8,128)(2,1)}, bf16[18,32,128]{2,1,0:T(8,128)(2,1)}, u32[]{:S(2)}, u32[]{:S(2)}) collective-permute-start(bf16[18,32,128]{2,1,0:T(8,128)(2,1)} %get-tuple-element.30), channel_id=1, source_target_pairs={{0,8},{1,9},{2,10},{3,11},{4,12},{5,13},{6,14},{7,15},{8,0},{9,1},... | collective-permute-start | bytes 442376 | tf_op jit(solution)/shard_map/ppermute | solution.py:645
  44.1 20.7 %collective-permute-start.14 = (bf16[18,128,128]{2,1,0:T(8,128)(2,1)}, bf16[18,128,128]{2,1,0:T(8,128)(2,1)}, u32[]{:S(2)}, u32[]{:S(2)}) collective-permute-start(bf16[18,128,128]{2,1,0:T(8,128)(2,1)} %get-tuple-element.32.refs_1_), channel_id=1, source_target_pairs={{1,2},{3,4},{5,6},{7,8},{9,10},{11,12},{13,14},{17,18},{19,20},{21... | collective-permute-start | bytes 1769480 | tf_op jit(solution)/shard_map/ppermute | solution.py:645
  59.8 5.0 %collective-permute-start.13 = (bf16[18,128,128]{2,1,0:T(8,128)(2,1)}, bf16[18,128,128]{2,1,0:T(8,128)(2,1)}, u32[]{:S(2)}, u32[]{:S(2)}) collective-permute-start(bf16[18,128,128]{2,1,0:T(8,128)(2,1)} %get-tuple-element.35.refs_5_.refs_1_), channel_id=1, source_target_pairs={{0,1},{1,0},{2,3},{3,2},{4,5},{5,4},{6,7},{7,6},{8,9},{9,8},{10,11... | collective-permute-start | bytes 1769480 | tf_op jit(solution)/shard_map/ppermute | solution.py:645
  60.0 4.8 %collective-permute-start.15 = (bf16[2240,128]{1,0:T(8,128)(2,1)}, bf16[2240,128]{1,0:T(8,128)(2,1)}, u32[]{:S(2)}, u32[]{:S(2)}) collective-permute-start(bf16[2240,128]{1,0:T(8,128)(2,1)} %get-tuple-element.36.refs_4_), channel_id=1, source_target_pairs={{0,1},{1,0},{2,3},{3,2},{4,5},{5,4},{6,7},{7,6},{8,9},{9,8},{10,11... | collective-permute-start | bytes 1720328 | tf_op jit(solution)/shard_map/ppermute | solution.py:645
